TPU v7x, 32 devices: a whole 2x2x4 slice. The times are simulated.
32 devices in a mesh: segment: 4 (over y, x), dp: 8 (over z, core).
Axes of the slice: x: 2, y: 2, z: 4, core: 2. Of those that a mesh axis runs over, the one named last changes fastest.
Arguments:
- stem: bfloat16 [32, 6, 6, 512], P('dp'), may hold values from -6 to 6
- labels: int32 [32], P('dp'), may hold values from 0 to 999
- cell_count: int32 [4], P('segment'), may hold values from 1 to 2, as said below
- pointwise: bfloat16 [8, 2, 512, 512], P('segment'), may hold values from -0.25 to 0.25
- depth_three: bfloat16 [8, 9, 512], P('segment'), may hold values from -2 to 2
- depth_five: bfloat16 [8, 25, 512], P('segment'), may hold values from -1.25 to 1.25
- classifier: bfloat16 [512, 1000], replicated, may hold values from -0.25 to 0.25
Outputs:
- grad_pointwise: float32 [8, 2, 512, 512], P('segment', None, None, 'dp')
- grad_three: float32 [8, 9, 512], P('segment', None, 'dp')
- grad_five: float32 [8, 25, 512], P('segment', None, 'dp')
Inputs may be any that keep to these rules, and one draw needn't show every extreme that they name: `cell_count`: some section runs 2 cells and some section runs one.
All inputs are finite; a program needn't handle non-finite values.
Results may differ from a plain program's by a relative error of at most 0.013.
Values may be sent and summed in bfloat16 or wider, within the bound.
No kernel may reach another device: no remote copies, remote signals or barrier semaphores. Data moves between devices by JAX's collectives and lax.ppermute only.
A program may use at most 128 MiB of HBM per device.

v0:
```python
import jax
import jax.numpy as jnp
from jax import lax
from jax.sharding import PartitionSpec as P

LOSS_SCALE = 256.0


def passed_along(value, axis, by):
    peers = lax.axis_size(axis)
    pairs = [(i, i + by) for i in range(peers) if 0 <= i + by < peers]
    return lax.ppermute(value, axis, pairs)


def depthwise(image, taps, width):
    reach = width // 2
    side = image.shape[0]
    padded = jnp.pad(image.astype(jnp.float32), ((reach, reach), (reach, reach), (0, 0)))
    total = jnp.zeros(image.shape, jnp.float32)
    for row in range(width):
        for column in range(width):
            total = (
                total
                + padded[row : row + side, column : column + side] * taps[row * width + column]
            )
    return total


def cell(pair, weight_pw, weight_three, weight_five):
    older, newer = (pair[0], pair[1])
    side, feat = (newer.shape[0], newer.shape[2])
    zero = jnp.zeros((), newer.dtype)
    branch_a = lax.optimization_barrier(
        depthwise(jnp.maximum(newer, zero), weight_three, 3).astype(jnp.bfloat16)
    )
    branch_b = lax.optimization_barrier(
        depthwise(jnp.maximum(older, zero), weight_five, 5).astype(jnp.bfloat16)
    )
    left = jnp.dot(branch_a.astype(jnp.float32).reshape(-1, feat), weight_pw[0])
    right = jnp.dot(branch_b.astype(jnp.float32).reshape(-1, feat), weight_pw[1])
    fresh = (left + right).reshape(side, side, feat).astype(jnp.bfloat16)
    return jnp.stack([newer, fresh])


def segment_run(pair, params, count):
    weight_pw, weight_three, weight_five = params
    for slot in range(weight_pw.shape[0]):
        pair = lax.cond(
            slot < count,
            lambda p, s=slot: cell(p, weight_pw[s], weight_three[s], weight_five[s]),
            lambda p: p,
            pair,
        )
    return pair


def head_loss(final, classifier, label):
    pooled = jnp.mean(final.astype(jnp.float32), axis=(0, 1))
    logits = jnp.dot(pooled, classifier.astype(jnp.float32), precision=lax.Precision.HIGHEST)
    target = (jnp.arange(logits.shape[0], dtype=jnp.int32) == label).astype(jnp.float32)
    return 0.5 * LOSS_SCALE * jnp.sum((logits - target) ** 2)


def per_device(stem, labels, cell_count, pointwise, depth_three, depth_five, classifier):
    segments = lax.axis_size("segment")
    here = lax.axis_index("segment")
    count = cell_count[0]
    params = (
        pointwise.astype(jnp.float32),
        depth_three.astype(jnp.float32),
        depth_five.astype(jnp.float32),
    )
    micro = stem.shape[0]
    ticks = micro + segments - 1
    pair_shape = (2,) + stem.shape[1:]
    empty_pair = jnp.zeros(pair_shape, jnp.bfloat16)

    def forward_tick(tick, carry):
        sent, inputs_buf, last_buf = carry
        received = passed_along(sent, "segment", 1)
        index = tick - here
        valid = (index >= 0) & (index < micro)
        clipped = jnp.clip(index, 0, micro - 1)
        image = lax.dynamic_index_in_dim(stem, clipped, 0, keepdims=False)
        entry = jnp.where(here == 0, jnp.stack([image, image]), received)
        result = lax.cond(valid, lambda p: segment_run(p, params, count), jnp.zeros_like, entry)
        old_entry = lax.dynamic_index_in_dim(inputs_buf, clipped, 0, keepdims=False)
        inputs_buf = lax.dynamic_update_index_in_dim(
            inputs_buf, jnp.where(valid, entry, old_entry), clipped, 0
        )
        old_last = lax.dynamic_index_in_dim(last_buf, clipped, 0, keepdims=False)
        last_buf = lax.dynamic_update_index_in_dim(
            last_buf, jnp.where(valid, result[1], old_last), clipped, 0
        )
        return (result, inputs_buf, last_buf)

    start = (
        empty_pair,
        jnp.zeros((micro,) + pair_shape, jnp.bfloat16),
        jnp.zeros(stem.shape, jnp.bfloat16),
    )
    _, inputs_buf, last_buf = lax.fori_loop(0, ticks, forward_tick, start)

    def head_cotangent(final, label):
        return jax.grad(head_loss)(final, classifier, label)

    top_grads = jax.vmap(head_cotangent)(last_buf, labels)

    def backward_tick(tick, carry):
        sent, grads = carry
        received = passed_along(sent, "segment", -1)
        index = tick - (segments - 1 - here)
        valid = (index >= 0) & (index < micro)
        clipped = jnp.clip(index, 0, micro - 1)
        top = lax.dynamic_index_in_dim(top_grads, clipped, 0, keepdims=False)
        incoming = jnp.where(here == segments - 1, jnp.stack([jnp.zeros_like(top), top]), received)
        entry = lax.dynamic_index_in_dim(inputs_buf, clipped, 0, keepdims=False)

        def pull_back(operands):
            pair_in, cotangent, totals = operands
            _, pullback = jax.vjp(lambda p, w: segment_run(p, w, count), pair_in, params)
            back_pair, back_params = pullback(cotangent)
            return (back_pair, jax.tree.map(lambda a, b: a + b, totals, back_params))

        def nothing(operands):
            return (jnp.zeros_like(operands[0]), operands[2])

        return lax.cond(valid, pull_back, nothing, (entry, incoming, grads))

    zero_grads = jax.tree.map(jnp.zeros_like, params)
    _, grads = lax.fori_loop(0, ticks, backward_tick, (empty_pair, zero_grads))
    feat = pointwise.shape[-1]
    slots = pointwise.shape[0]
    flat = (grads[0].reshape(-1, feat), grads[1].reshape(-1, feat), grads[2].reshape(-1, feat))
    share = feat // lax.axis_size("dp")
    summed = (
        lax.psum(flat[0].astype(jnp.bfloat16), "dp").astype(jnp.float32),
        lax.psum(flat[1].astype(jnp.bfloat16), "dp").astype(jnp.float32),
        lax.psum(flat[2].astype(jnp.bfloat16), "dp").astype(jnp.float32),
    )
    offset = lax.axis_index("dp") * share
    pieces = tuple((lax.dynamic_slice_in_dim(member, offset, share, 1) for member in summed))
    return (
        pieces[0].reshape(slots, 2, feat, share),
        pieces[1].reshape(slots, 9, share),
        pieces[2].reshape(slots, 25, share),
    )


def solution(mesh):
    return jax.shard_map(
        per_device,
        mesh=mesh,
        in_specs=(
            P("dp", None, None, None),
            P("dp"),
            P("segment"),
            P("segment", None, None, None),
            P("segment", None, None),
            P("segment", None, None),
            P(),
        ),
        out_specs=(
            P("segment", None, None, "dp"),
            P("segment", None, "dp"),
            P("segment", None, "dp"),
        ),
        check_vma=False,
    )
```

profile of v0, /device:TPU:0, one launch (start us, length us, event | category | flops | bytes accessed | tf_op | source)
XLA Modules:
  0.0 995.1 jit_solution(15927172027277334813)
XLA Ops:
  10.5 110.4 %while.40 = (s32[]{:T(128)}, bf16[2,6,6,512]{3,2,1,0:T(8,128)(2,1)S(1)}, bf16[4,2,6,6,512]{4,3,2,1,0:T(8,128)(2,1)S(1)}, bf16[4,6,6,512]{3,2,1,0:T(8,128)(2,1)S(...) while((s32[]{:T(128)}, ...), condition=%wide.region_7.8_spmd, body=%wide.region_0.7_spmd.sunk | while | flops 78538760 | bytes 5820842 | solution.py:102
  17.6 7.2 conditional.11
  37.2 10.5 %collective-permute-start = (bf16[2,6,6,512]{3,2,1,0:T(8,128)(2,1)S(1)}, bf16[2,6,6,512]{3,2,1,0:T(8,128)(2,1)S(1)}, u32[]{:S(2)}, u32[]{:S(2)}) collective-permute-start(bf16[2,6,6,512]{3,2,1,0:T(8,128)(2,1)S(1)} %get-tuple-element.2389), channel_id=1, source_target_pairs={{0,8},{8,16},{16,24},{1,9},{9,17},{17,25},{2,10},{10,18},{18,26},{... | collective-permute-start | bytes 221192 | tf_op jit(solution)/shard_map/while/body/eval_jaxpr/ppermute | solution.py:12
  57.9 10.5 %collective-permute-start = (bf16[2,6,6,512]{3,2,1,0:T(8,128)(2,1)S(1)}, bf16[2,6,6,512]{3,2,1,0:T(8,128)(2,1)S(1)}, u32[]{:S(2)}, u32[]{:S(2)}) collective-permute-start(bf16[2,6,6,512]{3,2,1,0:T(8,128)(2,1)S(1)} %get-tuple-element.2389), channel_id=1, source_target_pairs={{0,8},{8,16},{16,24},{1,9},{9,17},{17,25},{2,10},{10,18},{18,26},{... | collective-permute-start | bytes 221192 | tf_op jit(solution)/shard_map/while/body/eval_jaxpr/ppermute | solution.py:12
  78.6 10.5 %collective-permute-start = (bf16[2,6,6,512]{3,2,1,0:T(8,128)(2,1)S(1)}, bf16[2,6,6,512]{3,2,1,0:T(8,128)(2,1)S(1)}, u32[]{:S(2)}, u32[]{:S(2)}) collective-permute-start(bf16[2,6,6,512]{3,2,1,0:T(8,128)(2,1)S(1)} %get-tuple-element.2389), channel_id=1, source_target_pairs={{0,8},{8,16},{16,24},{1,9},{9,17},{17,25},{2,10},{10,18},{18,26},{... | collective-permute-start | bytes 221192 | tf_op jit(solution)/shard_map/while/body/eval_jaxpr/ppermute | solution.py:12
  92.1 17.8 %collective-permute-start = (bf16[2,6,6,512]{3,2,1,0:T(8,128)(2,1)S(1)}, bf16[2,6,6,512]{3,2,1,0:T(8,128)(2,1)S(1)}, u32[]{:S(2)}, u32[]{:S(2)}) collective-permute-start(bf16[2,6,6,512]{3,2,1,0:T(8,128)(2,1)S(1)} %get-tuple-element.2389), channel_id=1, source_target_pairs={{0,8},{8,16},{16,24},{1,9},{9,17},{17,25},{2,10},{10,18},{18,26},{... | collective-permute-start | bytes 221192 | tf_op jit(solution)/shard_map/while/body/eval_jaxpr/ppermute | solution.py:12
  126.2 738.3 %while.41 = (s32[]{:T(128)}, bf16[2,6,6,512]{3,2,1,0:T(8,128)(2,1)}, f32[2,2,512,512]{3,2,1,0:T(8,128)}, f32[2,9,512]{2,1,0:T(8,128)S(1)}, f32[2,25,512]{2,1,0:T...) while((s32[]{:T(128)}, ...), condition=%wide.region_88.89_spmd.clone, body=%wide.region_9.88_spmd.clone.sunk | while | flops 202348544 | bytes 82573848 | solution.py:131
  127.5 11.5 %collective-permute-done.1 = bf16[2,6,6,512]{3,2,1,0:T(8,128)(2,1)S(1)} collective-permute-done((bf16[2,6,6,512]{3,2,1,0:T(8,128)(2,1)}, bf16[2,6,6,512]{3,2,1,0:T(8,128)(2,1)S(1)}, u32[]{:S(2)}, u32[]{:S(2)}) %collective-permute-start.1) | collective-permute-done | bytes 73760 | tf_op jit(solution)/shard_map/while/body/eval_jaxpr/ppermute | solution.py:12
  148.8 15.3 %collective-permute-done.1 = bf16[2,6,6,512]{3,2,1,0:T(8,128)(2,1)S(1)} collective-permute-done((bf16[2,6,6,512]{3,2,1,0:T(8,128)(2,1)}, bf16[2,6,6,512]{3,2,1,0:T(8,128)(2,1)S(1)}, u32[]{:S(2)}, u32[]{:S(2)}) %collective-permute-start.1) | collective-permute-done | bytes 73760 | tf_op jit(solution)/shard_map/while/body/eval_jaxpr/ppermute | solution.py:12
  166.1 271.4 %collective-permute-done.1 = bf16[2,6,6,512]{3,2,1,0:T(8,128)(2,1)S(1)} collective-permute-done((bf16[2,6,6,512]{3,2,1,0:T(8,128)(2,1)}, bf16[2,6,6,512]{3,2,1,0:T(8,128)(2,1)S(1)}, u32[]{:S(2)}, u32[]{:S(2)}) %collective-permute-start.1) | collective-permute-done | bytes 73760 | tf_op jit(solution)/shard_map/while/body/eval_jaxpr/ppermute | solution.py:12
  437.5 101.7 %conditional.12 = (bf16[2,6,6,512]{3,2,1,0:T(8,128)(2,1)}, f32[2,2,512,512]{3,2,1,0:T(8,128)}, f32[2,9,512]{2,1,0:T(8,128)S(1)}, f32[2,25,512]{2,1,0:T(8,128)S(1)}) conditional(s32[]{:T(128)} %convert_element_type.565, (f32[2,2,512,512]{3,2,1,0:T(8,128)}, f32[2,9,512]{2,1,0:T(8,128)S(1)}, f32[2,25,512]{2,1,0:T(8,128)S(1)}) %tuple.550, (s32[]{:T(128)}, ...), branch_computations={%region_10.10_spmd, %region_11.87_spmd} | conditional | flops 202348544 | bytes 82278584 | solution.py:128
  441.0 18.4 %conditional.3 = (bf16[2,6,6,512]{3,2,1,0:T(8,128)(2,1)S(1)}, bf16[6,6,512]{2,1,0:T(8,128)(2,1)}, f32[1,1,512]{2,1,0:T(1,128)}, f32[6,6,512]{2,1,0:T(8,128)}, f3...) conditional(s32[]{:T(128)} %convert_element_type.225, ...), branch_computations={%region_12.11_spmd, %region_13.12_spmd} | conditional | flops 39297024 | bytes 6894168 | solution.py:48
  460.2 45.2 %conditional.4 = (bf16[6,6,512]{2,1,0:T(8,128)(2,1)}, f32[1,1,512]{2,1,0:T(1,128)}, f32[6,6,512]{2,1,0:T(8,128)}, f32[1,1,512]{2,1,0:T(1,128)}, f32[6,6,512]{2,1...) conditional(s32[]{:T(128)} %convert_element_type.226, ...), branch_computations={%region_14.13_spmd, %region_15.14_spmd} | conditional | flops 1474560 | bytes 5329488 | solution.py:48
  508.5 19.1 %conditional.6 = (f32[2,2,512,512]{3,2,1,0:T(8,128)}, f32[2,9,512]{2,1,0:T(8,128)}, f32[2,25,512]{2,1,0:T(8,128)S(1)}, bf16[2,6,6,512]{3,2,1,0:T(8,128)(2,1)}) conditional(s32[]{:T(128)} %convert_element_type.225, bf16[2,6,6,512]{3,2,1,0:T(8,128)(2,1)} %get-tuple-element.1237, (bf16[2,6,6,512]{3,2,1,0:T(8,128)(2,1)}, bf16[36,512]{1,0:T(8,128)(2,1)}, ...), branch_computations={%region_52.51_spmd, %region_53.86_spmd} | conditional | flops 79686656 | bytes 25805096 | solution.py:48
  530.8 8.4 add_add_fusion
  545.9 101.7 %conditional.12 = (bf16[2,6,6,512]{3,2,1,0:T(8,128)(2,1)}, f32[2,2,512,512]{3,2,1,0:T(8,128)}, f32[2,9,512]{2,1,0:T(8,128)S(1)}, f32[2,25,512]{2,1,0:T(8,128)S(1)}) conditional(s32[]{:T(128)} %convert_element_type.565, (f32[2,2,512,512]{3,2,1,0:T(8,128)}, f32[2,9,512]{2,1,0:T(8,128)S(1)}, f32[2,25,512]{2,1,0:T(8,128)S(1)}) %tuple.550, (s32[]{:T(128)}, ...), branch_computations={%region_10.10_spmd, %region_11.87_spmd} | conditional | flops 202348544 | bytes 82278584 | solution.py:128
  549.5 18.4 %conditional.3 = (bf16[2,6,6,512]{3,2,1,0:T(8,128)(2,1)S(1)}, bf16[6,6,512]{2,1,0:T(8,128)(2,1)}, f32[1,1,512]{2,1,0:T(1,128)}, f32[6,6,512]{2,1,0:T(8,128)}, f3...) conditional(s32[]{:T(128)} %convert_element_type.225, ...), branch_computations={%region_12.11_spmd, %region_13.12_spmd} | conditional | flops 39297024 | bytes 6894168 | solution.py:48
  568.6 45.2 %conditional.4 = (bf16[6,6,512]{2,1,0:T(8,128)(2,1)}, f32[1,1,512]{2,1,0:T(1,128)}, f32[6,6,512]{2,1,0:T(8,128)}, f32[1,1,512]{2,1,0:T(1,128)}, f32[6,6,512]{2,1...) conditional(s32[]{:T(128)} %convert_element_type.226, ...), branch_computations={%region_14.13_spmd, %region_15.14_spmd} | conditional | flops 1474560 | bytes 5329488 | solution.py:48
  616.9 19.1 %conditional.6 = (f32[2,2,512,512]{3,2,1,0:T(8,128)}, f32[2,9,512]{2,1,0:T(8,128)}, f32[2,25,512]{2,1,0:T(8,128)S(1)}, bf16[2,6,6,512]{3,2,1,0:T(8,128)(2,1)}) conditional(s32[]{:T(128)} %convert_element_type.225, bf16[2,6,6,512]{3,2,1,0:T(8,128)(2,1)} %get-tuple-element.1237, (bf16[2,6,6,512]{3,2,1,0:T(8,128)(2,1)}, bf16[36,512]{1,0:T(8,128)(2,1)}, ...), branch_computations={%region_52.51_spmd, %region_53.86_spmd} | conditional | flops 79686656 | bytes 25805096 | solution.py:48
  639.2 8.4 add_add_fusion
  654.3 101.7 %conditional.12 = (bf16[2,6,6,512]{3,2,1,0:T(8,128)(2,1)}, f32[2,2,512,512]{3,2,1,0:T(8,128)}, f32[2,9,512]{2,1,0:T(8,128)S(1)}, f32[2,25,512]{2,1,0:T(8,128)S(1)}) conditional(s32[]{:T(128)} %convert_element_type.565, (f32[2,2,512,512]{3,2,1,0:T(8,128)}, f32[2,9,512]{2,1,0:T(8,128)S(1)}, f32[2,25,512]{2,1,0:T(8,128)S(1)}) %tuple.550, (s32[]{:T(128)}, ...), branch_computations={%region_10.10_spmd, %region_11.87_spmd} | conditional | flops 202348544 | bytes 82278584 | solution.py:128
  657.9 18.4 %conditional.3 = (bf16[2,6,6,512]{3,2,1,0:T(8,128)(2,1)S(1)}, bf16[6,6,512]{2,1,0:T(8,128)(2,1)}, f32[1,1,512]{2,1,0:T(1,128)}, f32[6,6,512]{2,1,0:T(8,128)}, f3...) conditional(s32[]{:T(128)} %convert_element_type.225, ...), branch_computations={%region_12.11_spmd, %region_13.12_spmd} | conditional | flops 39297024 | bytes 6894168 | solution.py:48
  677.0 45.2 %conditional.4 = (bf16[6,6,512]{2,1,0:T(8,128)(2,1)}, f32[1,1,512]{2,1,0:T(1,128)}, f32[6,6,512]{2,1,0:T(8,128)}, f32[1,1,512]{2,1,0:T(1,128)}, f32[6,6,512]{2,1...) conditional(s32[]{:T(128)} %convert_element_type.226, ...), branch_computations={%region_14.13_spmd, %region_15.14_spmd} | conditional | flops 1474560 | bytes 5329488 | solution.py:48
  725.4 19.1 %conditional.6 = (f32[2,2,512,512]{3,2,1,0:T(8,128)}, f32[2,9,512]{2,1,0:T(8,128)}, f32[2,25,512]{2,1,0:T(8,128)S(1)}, bf16[2,6,6,512]{3,2,1,0:T(8,128)(2,1)}) conditional(s32[]{:T(128)} %convert_element_type.225, bf16[2,6,6,512]{3,2,1,0:T(8,128)(2,1)} %get-tuple-element.1237, (bf16[2,6,6,512]{3,2,1,0:T(8,128)(2,1)}, bf16[36,512]{1,0:T(8,128)(2,1)}, ...), branch_computations={%region_52.51_spmd, %region_53.86_spmd} | conditional | flops 79686656 | bytes 25805096 | solution.py:48
  747.6 8.4 add_add_fusion
  762.7 101.7 %conditional.12 = (bf16[2,6,6,512]{3,2,1,0:T(8,128)(2,1)}, f32[2,2,512,512]{3,2,1,0:T(8,128)}, f32[2,9,512]{2,1,0:T(8,128)S(1)}, f32[2,25,512]{2,1,0:T(8,128)S(1)}) conditional(s32[]{:T(128)} %convert_element_type.565, (f32[2,2,512,512]{3,2,1,0:T(8,128)}, f32[2,9,512]{2,1,0:T(8,128)S(1)}, f32[2,25,512]{2,1,0:T(8,128)S(1)}) %tuple.550, (s32[]{:T(128)}, ...), branch_computations={%region_10.10_spmd, %region_11.87_spmd} | conditional | flops 202348544 | bytes 82278584 | solution.py:128
  766.3 18.4 %conditional.3 = (bf16[2,6,6,512]{3,2,1,0:T(8,128)(2,1)S(1)}, bf16[6,6,512]{2,1,0:T(8,128)(2,1)}, f32[1,1,512]{2,1,0:T(1,128)}, f32[6,6,512]{2,1,0:T(8,128)}, f3...) conditional(s32[]{:T(128)} %convert_element_type.225, ...), branch_computations={%region_12.11_spmd, %region_13.12_spmd} | conditional | flops 39297024 | bytes 6894168 | solution.py:48
  785.5 45.2 %conditional.4 = (bf16[6,6,512]{2,1,0:T(8,128)(2,1)}, f32[1,1,512]{2,1,0:T(1,128)}, f32[6,6,512]{2,1,0:T(8,128)}, f32[1,1,512]{2,1,0:T(1,128)}, f32[6,6,512]{2,1...) conditional(s32[]{:T(128)} %convert_element_type.226, ...), branch_computations={%region_14.13_spmd, %region_15.14_spmd} | conditional | flops 1474560 | bytes 5329488 | solution.py:48
  833.8 19.1 %conditional.6 = (f32[2,2,512,512]{3,2,1,0:T(8,128)}, f32[2,9,512]{2,1,0:T(8,128)}, f32[2,25,512]{2,1,0:T(8,128)S(1)}, bf16[2,6,6,512]{3,2,1,0:T(8,128)(2,1)}) conditional(s32[]{:T(128)} %convert_element_type.225, bf16[2,6,6,512]{3,2,1,0:T(8,128)(2,1)} %get-tuple-element.1237, (bf16[2,6,6,512]{3,2,1,0:T(8,128)(2,1)}, bf16[36,512]{1,0:T(8,128)(2,1)}, ...), branch_computations={%region_52.51_spmd, %region_53.86_spmd} | conditional | flops 79686656 | bytes 25805096 | solution.py:48
  856.1 8.4 add_add_fusion
  870.8 44.5 %all-reduce.165.cloned.1.call-done = (bf16[18,512]{1,0:T(8,128)(2,1)}, bf16[50,512]{1,0:T(8,128)(2,1)}) async-done(((bf16[18,512]{1,0:T(8,128)(2,1)}, bf16[50,512]{1,0:T(8,128)(2,1)}), (bf16[18,512]{1,0:T(8,128)(2,1)}, bf16[50,512]{1,0:T(8,128)(2,1)})) %all-reduce.165.cloned.1.call-update) | async-done | bytes 69648 | tf_op jit(solution)/shard_map/psum | solution.py:138
  918.1 67.8 %all-reduce.163.cloned.1.call-done = bf16[2048,512]{0,1:T(8,128)(2,1)} async-done(((bf16[2048,512]{0,1:T(8,128)(2,1)}), bf16[2048,512]{0,1:T(8,128)(2,1)}) %all-reduce.163.cloned.1.call-update) | async-done | bytes 2097168 | tf_op jit(solution)/shard_map/psum | solution.py:137
  (757 shorter events, 536.3 us)
Async XLA Ops:
  7.2 113.8 %copy-start = (bf16[512,1000]{0,1:T(8,128)(2,1)S(1)}, bf16[512,1000]{0,1:T(8,128)(2,1)}, u32[]{:S(2)}) copy-start(bf16[512,1000]{0,1:T(8,128)(2,1)} %param.33) | copy-start | bytes 3072004
  7.2 908.1 %all-reduce.165.cloned.1.call-start = ((), (), s32[]{:S(2)}) async-start(), calls=%async_computation.1 | async-start | bytes 163840 | tf_op jit(solution)/shard_map/psum | solution.py:138
  10.5 110.5 %copy-start.26 = (s32[4]{0:T(128)S(1)}, s32[4]{0:T(128)}, u32[]{:S(2)}) copy-start(s32[4]{0:T(128)} %param.28) | copy-start | bytes 52
  10.6 7.0 collective-permute-start
  25.6 3.5 collective-permute-start
  37.2 12.7 %collective-permute-start = (bf16[2,6,6,512]{3,2,1,0:T(8,128)(2,1)S(1)}, bf16[2,6,6,512]{3,2,1,0:T(8,128)(2,1)S(1)}, u32[]{:S(2)}, u32[]{:S(2)}) collective-permute-start(bf16[2,6,6,512]{3,2,1,0:T(8,128)(2,1)S(1)} %get-tuple-element.2389), channel_id=1, source_target_pairs={{0,8},{8,16},{16,24},{1,9},{9,17},{17,25},{2,10},{10,18},{18,26},{... | collective-permute-start | bytes 221192 | tf_op jit(solution)/shard_map/while/body/eval_jaxpr/ppermute | solution.py:12
  57.9 12.7 %collective-permute-start = (bf16[2,6,6,512]{3,2,1,0:T(8,128)(2,1)S(1)}, bf16[2,6,6,512]{3,2,1,0:T(8,128)(2,1)S(1)}, u32[]{:S(2)}, u32[]{:S(2)}) collective-permute-start(bf16[2,6,6,512]{3,2,1,0:T(8,128)(2,1)S(1)} %get-tuple-element.2389), channel_id=1, source_target_pairs={{0,8},{8,16},{16,24},{1,9},{9,17},{17,25},{2,10},{10,18},{18,26},{... | collective-permute-start | bytes 221192 | tf_op jit(solution)/shard_map/while/body/eval_jaxpr/ppermute | solution.py:12
  78.6 12.7 %collective-permute-start = (bf16[2,6,6,512]{3,2,1,0:T(8,128)(2,1)S(1)}, bf16[2,6,6,512]{3,2,1,0:T(8,128)(2,1)S(1)}, u32[]{:S(2)}, u32[]{:S(2)}) collective-permute-start(bf16[2,6,6,512]{3,2,1,0:T(8,128)(2,1)S(1)} %get-tuple-element.2389), channel_id=1, source_target_pairs={{0,8},{8,16},{16,24},{1,9},{9,17},{17,25},{2,10},{10,18},{18,26},{... | collective-permute-start | bytes 221192 | tf_op jit(solution)/shard_map/while/body/eval_jaxpr/ppermute | solution.py:12
  92.1 20.7 %collective-permute-start = (bf16[2,6,6,512]{3,2,1,0:T(8,128)(2,1)S(1)}, bf16[2,6,6,512]{3,2,1,0:T(8,128)(2,1)S(1)}, u32[]{:S(2)}, u32[]{:S(2)}) collective-permute-start(bf16[2,6,6,512]{3,2,1,0:T(8,128)(2,1)S(1)} %get-tuple-element.2389), channel_id=1, source_target_pairs={{0,8},{8,16},{16,24},{1,9},{9,17},{17,25},{2,10},{10,18},{18,26},{... | collective-permute-start | bytes 221192 | tf_op jit(solution)/shard_map/while/body/eval_jaxpr/ppermute | solution.py:12
  113.6 6.6 collective-permute-start
  126.2 12.8 %collective-permute-start.1 = (bf16[2,6,6,512]{3,2,1,0:T(8,128)(2,1)}, bf16[2,6,6,512]{3,2,1,0:T(8,128)(2,1)S(1)}, u32[]{:S(2)}, u32[]{:S(2)}) collective-permute-start(bf16[2,6,6,512]{3,2,1,0:T(8,128)(2,1)} %get-tuple-element.2435), channel_id=1, source_target_pairs={{8,0},{16,8},{24,16},{9,1},{17,9},{25,17},{10,2},{18,10},{26,18},{... | collective-permute-start | bytes 221192 | tf_op jit(solution)/shard_map/while/body/eval_jaxpr/ppermute | solution.py:12
  139.6 7.2 collective-permute-start.1
  147.5 16.6 %collective-permute-start.1 = (bf16[2,6,6,512]{3,2,1,0:T(8,128)(2,1)}, bf16[2,6,6,512]{3,2,1,0:T(8,128)(2,1)S(1)}, u32[]{:S(2)}, u32[]{:S(2)}) collective-permute-start(bf16[2,6,6,512]{3,2,1,0:T(8,128)(2,1)} %get-tuple-element.2435), channel_id=1, source_target_pairs={{8,0},{16,8},{24,16},{9,1},{17,9},{25,17},{10,2},{18,10},{26,18},{... | collective-permute-start | bytes 221192 | tf_op jit(solution)/shard_map/while/body/eval_jaxpr/ppermute | solution.py:12
  164.8 272.7 %collective-permute-start.1 = (bf16[2,6,6,512]{3,2,1,0:T(8,128)(2,1)}, bf16[2,6,6,512]{3,2,1,0:T(8,128)(2,1)S(1)}, u32[]{:S(2)}, u32[]{:S(2)}) collective-permute-start(bf16[2,6,6,512]{3,2,1,0:T(8,128)(2,1)} %get-tuple-element.2435), channel_id=1, source_target_pairs={{8,0},{16,8},{24,16},{9,1},{17,9},{25,17},{10,2},{18,10},{26,18},{... | collective-permute-start | bytes 221192 | tf_op jit(solution)/shard_map/while/body/eval_jaxpr/ppermute | solution.py:12
  508.5 6.3 copy-start.14
  508.5 6.3 copy-start.16
  530.8 8.4 copy-start.20
  530.8 8.4 copy-start.24
  539.2 6.7 collective-permute-start.1
  616.9 6.3 copy-start.14
  616.9 6.3 copy-start.16
  639.2 8.4 copy-start.20
  639.2 8.4 copy-start.24
  647.6 6.7 collective-permute-start.1
  725.4 6.3 copy-start.16
  747.6 8.4 copy-start.20
  747.6 8.4 copy-start.24
  756.0 6.7 collective-permute-start.1
  833.8 6.3 copy-start.16
  856.1 8.4 copy-start.20
  856.1 8.4 copy-start.24
  865.7 120.2 %all-reduce.163.cloned.1.call-start = ((), (), s32[]{:S(2)}) async-start(), calls=%async_computation | async-start | bytes 4194304 | tf_op jit(solution)/shard_map/psum | solution.py:137
  (53 other events, 108.7 us)
Sparse Core Ops, SparseCore 0:
  865.9 49.3 all-reduce.164
  917.8 68.1 all-reduce.162
where the time goes:
time: 1010 us; the launch traced here: 995 us
  waiting for transfers between devices  448 us (44%)
  local copies, waits for them, and re-layouts  277 us (27%)
  other arithmetic  133 us (13%)
  starting transfers between devices  68.8 us (7%)
  matrix products  41.7 us (4%)
  between operations  14.2 us (1%)
  loops' own time  12.7 us (1%)
    ppermute x14, waiting for transfers between devices, passed_along(): return lax.ppermute(value, axis, pairs)  336 us
    another operation x319, local copies, waits for them, and re-layouts  198 us
    ppermute x14, starting transfers between devices, passed_along(): return lax.ppermute(value, axis, pairs)  68.7 us
    psum x1, waiting for transfers between devices, per_device(): lax.psum(flat[0].astype(jnp.bfloat16), 'dp').astype(jnp.float32)  67.8 us
    add x12, other arithmetic, pull_back(): return (back_pair, jax.tree.map(lambda a, b: a + b, totals, back_params))  46 us
    psum x1, waiting for transfers between devices, per_device(): lax.psum(flat[1].astype(jnp.bfloat16), 'dp').astype(jnp.float32)  44.5 us
    slice x16, local copies, waits for them, and re-layouts, depthwise(): taps[row * width + column]  23.8 us
  transfers between devices with their start and end apart: 16, of which 16 were waited for; matrix products, arithmetic and copies ran while one was open for 1% of the time, Pallas kernels for 0%

commit v1 on v0

v1 whole, which is shorter than its diff:
```python
import functools

import jax
import jax.numpy as jnp
from jax import lax
from jax.experimental import pallas as pl
from jax.experimental.pallas import tpu as pltpu
from jax.sharding import PartitionSpec as P

LOSS_SCALE = 256.0
SUB = 8
LANE = 128
BF = jnp.bfloat16
F32 = jnp.float32


class Dims:
    def __init__(self, images, side, feat):
        self.n = images
        self.side = side
        self.feat = feat
        self.parts = SUB // images
        self.tiles = feat // (self.parts * LANE)
        self.pos = side * side
        self.pad = -(-self.pos // SUB) * SUB
        self.rows = self.pos * SUB
        self.rows_pad = self.pad * SUB
        self.flat = images * self.pad

    def lanes(self, part, tile):
        start = (part * self.tiles + tile) * LANE
        return slice(start, start + LANE)


def valid_taps(side, width, y, x, sign):
    reach = width // 2
    found = []
    for row in range(width):
        for column in range(width):
            yy = y + sign * (row - reach)
            xx = x + sign * (column - reach)
            if 0 <= yy < side and 0 <= xx < side:
                found.append((row * width + column, yy * side + xx))
    return found


def spread_taps(d, source, slot, taps_ref):
    for tap in range(source.shape[0]):
        value = source[tap, slot : slot + 1]
        for part in range(d.parts):
            for tile in range(d.tiles):
                start = tap * SUB + part * d.n
                taps_ref[tile, start : start + d.n, :] = jnp.broadcast_to(
                    value[:, d.lanes(part, tile)], (d.n, LANE)
                )


def conv(d, x_ref, taps_ref, width, sign, emit):
    first = 0 if width == 3 else 9
    for tile in range(d.tiles):
        for y in range(d.side):
            for x in range(d.side):
                total = None
                for tap, at in valid_taps(d.side, width, y, x, sign):
                    w = taps_ref[tile, (first + tap) * SUB : (first + tap + 1) * SUB, :]
                    v = x_ref[tile, at * SUB : (at + 1) * SUB, :] * w
                    total = v if total is None else total + v
                emit(tile, y * d.side + x, total)


def to_rows(d, ref):
    images = []
    for image in range(d.n):
        pieces = []
        for part in range(d.parts):
            for tile in range(d.tiles):
                pieces.append(ref[tile, pl.ds(part * d.n + image, d.pad, stride=SUB), :])
        images.append(jnp.concatenate(pieces, axis=1))
    return jnp.concatenate(images, axis=0) if d.n > 1 else images[0]


def from_rows(d, value, ref):
    for image in range(d.n):
        for part in range(d.parts):
            for tile in range(d.tiles):
                ref[tile, pl.ds(part * d.n + image, d.pad, stride=SUB), :] = value[
                    image * d.pad : (image + 1) * d.pad, d.lanes(part, tile)
                ]


def at(position):
    return slice(position * SUB, (position + 1) * SUB)


def clear_tail(d, ref):
    ref[:, d.rows :, :] = jnp.zeros((d.tiles, d.rows_pad - d.rows, LANE), F32)


def branch_rows(d, value, width, taps, xs, cs):
    xs[...] = jnp.maximum(value.astype(F32), 0.0)

    def emit(tile, position, v):
        cs[tile, at(position), :] = v

    conv(d, xs, taps, width, 1, emit)
    return to_rows(d, cs).astype(BF)


def forward_cell(d, older, newer, slot, w, table, scr):
    taps, xs, cs = scr["taps"], scr["xs"], scr["cs"]
    spread_taps(d, table, slot, taps)
    rows_three = branch_rows(d, newer, 3, taps, xs, cs)
    rows_five = branch_rows(d, older, 5, taps, xs, cs)
    total = jnp.dot(rows_three, w[slot, 0], preferred_element_type=F32)
    total = total + jnp.dot(rows_five, w[slot, 1], preferred_element_type=F32)
    from_rows(d, total, cs)
    return cs[:, : d.rows, :].astype(BF)


def forward_section(d, count, w, table, res, last, scr):
    first = forward_cell(d, res[0], res[1], 0, w, table, scr)
    res[2] = first

    @pl.when(count > 1)
    def _():
        last[...] = forward_cell(d, res[1], res[2], 1, w, table, scr)

    @pl.when(count <= 1)
    def _():
        last[...] = res[2]


def slope(value):
    value = value.astype(F32)
    return jnp.where(value > 0, 1.0, jnp.where(value == 0, 0.5, 0.0))


def rounded(value):
    return value.astype(BF).astype(F32)


NT = (((1,), (1,)), ((), ()))
TN = (((0,), (0,)), ((), ()))


def backward_cell(d, slot, older, newer, w, table, scr, keep, cot, add_newer, out_newer, out_older, through=True):
    taps, xs, cs = scr["taps"], scr["xs"], scr["cs"]
    if through:
        spread_taps(d, table, slot, taps)
    rows = to_rows(d, cs).astype(BF)
    keep(slot, rows)
    for branch, width in ((0, 3), (1, 5)):
        back = lax.dot_general(rows, w[slot, branch], NT, preferred_element_type=F32)
        from_rows(d, rounded(back), cs)
        cot[2 * slot + branch] = cs[:, : d.rows, :].astype(BF)
        if not through:
            continue
        if branch == 0:

            def emit(tile, position, v):
                s = slope(newer[tile, at(position), :])
                xs[tile, at(position), :] = rounded(v) * s

            conv(d, cs, taps, 3, -1, emit)
            out_newer[...] = rounded(add_newer() + xs[...])
        else:

            def emit(tile, position, v):
                s = slope(older[tile, at(position), :])
                out_older[tile, at(position), :] = rounded(v) * s

            conv(d, cs, taps, 5, -1, emit)


def backward_section(d, info, w, table, res, blocks, cot, scr, out):
    cs, g0, g1, g2 = scr["cs"], scr["g0"], scr["g1"], scr["g2"]
    clear_tail(d, cs)
    count, place = info[1], info[2]
    depth, _, share = blocks.shape

    def keep(slot, rows):
        for other in range(depth):
            blocks[place ^ other, slot * d.flat : (slot + 1) * d.flat, :] = rows[
                :, other * share : (other + 1) * share
            ]

    @pl.when(count > 1)
    def _():
        cs[:, : d.rows, :] = g1[...]
        backward_cell(
            d, 1, res.at[1], res.at[2], w, table, scr, keep, cot, lambda: g0[...], g1, g2
        )

    @pl.when(count <= 1)
    def _():
        g2[...] = g0[...]
        blocks[:, d.flat : 2 * d.flat, :] = jnp.zeros((depth, d.flat, share), BF)
        cot[2] = jnp.zeros(cot.shape[1:], BF)
        cot[3] = jnp.zeros(cot.shape[1:], BF)

    cs[:, : d.rows, :] = g1[...]
    backward_cell(
        d, 0, res.at[0], res.at[1], w, table, scr, keep, cot, lambda: g2[...], g1, g0,
        through=out is not None,
    )
    if out is not None:
        out[0] = g0[...].astype(BF)
        out[1] = g1[...].astype(BF)


def head(d, final, label_ref, offset, classifier_ref, scr):
    g0, g1, hs = scr["g0"], scr["g1"], scr["hs"]
    for tile in range(d.tiles):
        total = None
        for position in range(d.pos):
            v = final[tile, at(position), :].astype(F32)
            total = v if total is None else total + v
        hs[tile] = total * (1.0 / d.pos)
    pieces = []
    for part in range(d.parts):
        for tile in range(d.tiles):
            pieces.append(hs[tile, part * d.n : (part + 1) * d.n, :])
    pooled = jnp.concatenate(pieces, axis=1)
    pooled = jnp.concatenate([pooled, jnp.zeros((SUB - d.n, d.feat), F32)], axis=0)

    def split(v):
        high = rounded(v)
        mid = rounded(v - high)
        low = v - high - mid
        return jnp.concatenate([high, mid, low, jnp.zeros_like(v)], axis=0).astype(BF)

    def joined(v):
        return v[0:SUB] + v[SUB : 2 * SUB] + v[2 * SUB : 3 * SUB]

    logits = joined(
        lax.dot_general(split(pooled), classifier_ref[...], NT, preferred_element_type=F32)
    )
    row = lax.broadcasted_iota(jnp.int32, logits.shape, 0)
    column = lax.broadcasted_iota(jnp.int32, logits.shape, 1)
    wanted = jnp.full(logits.shape, -1, jnp.int32)
    for image in range(d.n):
        wanted = jnp.where(row == image, label_ref[offset + image], wanted)
    target = jnp.where(column == wanted, 1.0, 0.0)
    back = LOSS_SCALE * (logits - target)
    pooled_cot = joined(
        jnp.dot(split(back), classifier_ref[...], preferred_element_type=F32)
    )
    each = rounded(pooled_cot * (1.0 / d.pos))
    for part in range(d.parts):
        for tile in range(d.tiles):
            hs[tile, part * d.n : (part + 1) * d.n, :] = each[: d.n, d.lanes(part, tile)]
    for tile in range(d.tiles):
        value = hs[tile]
        for position in range(d.pos):
            g1[tile, at(position), :] = value
    g0[...] = jnp.zeros(g0.shape, F32)


def load_stem(d, stem, chunk, cs):
    for y in range(d.side):
        for x in range(d.side):
            value = stem[y, x, chunk * d.n : (chunk + 1) * d.n]
            for part in range(d.parts):
                for tile in range(d.tiles):
                    start = (y * d.side + x) * SUB + part * d.n
                    cs[tile, start : start + d.n, :] = value[:, d.lanes(part, tile)]


SCRATCH = ("taps", "xs", "cs", "g0", "g1", "g2", "hs")


def scratch_shapes(d, n_taps):
    packed = (d.tiles, d.rows, LANE)
    return [
        pltpu.VMEM((d.tiles, n_taps * SUB, LANE), F32),
        pltpu.VMEM(packed, F32),
        pltpu.VMEM((d.tiles, d.rows_pad, LANE), F32),
        pltpu.VMEM(packed, F32),
        pltpu.VMEM(packed, F32),
        pltpu.VMEM(packed, F32),
        pltpu.VMEM((d.tiles, SUB, LANE), F32),
    ]


def hand_on(count, res, out):
    @pl.when(count > 1)
    def _():
        out[0] = res[2]

    @pl.when(count <= 1)
    def _():
        out[0] = res[1]


def take_stem(d, chunk, stem, res, scr):
    load_stem(d, stem, chunk, scr["cs"])
    value = scr["cs"][:, : d.rows, :].astype(BF)
    res[0] = value
    res[1] = value


def forward_kernel(d, chunk, step, info, pair, w, table, own_in, out, res, own, *rest):
    sems, scr = rest[-1], dict(zip(SCRATCH, rest))

    @pl.when(info[0] == step[0])
    def _():
        count = info[1]
        clear_tail(d, scr["cs"])
        if own_in is None:
            take_stem(d, chunk, pair, res, scr)
        else:
            res[0] = pair[0]
            res[1] = pair[1]
        copy = pltpu.make_async_copy(res.at[pl.ds(0, 2)], own, sems.at[0])
        copy.start()
        forward_section(d, count, w, table, res, out.at[1], scr)
        hand_on(count, res, out)
        copy.wait()


def fresh_kernel(d, chunk, step, info, stem, w, table, *rest):
    forward_kernel(d, chunk, step, info, stem, w, table, None, *rest)


def backward_kernel(d, step, info, cotangent, w, table, res, blocks_in, cot_in, out, blocks, cot, *rest):
    scr = dict(zip(SCRATCH, rest))

    @pl.when(info[0] == step[0])
    def _():
        scr["g0"][...] = cotangent[0].astype(F32)
        scr["g1"][...] = cotangent[1].astype(F32)
        backward_section(d, info, w, table, res, blocks, cot, scr, out)

    @pl.when(info[0] != step[0])
    def _():
        blocks[...] = blocks_in[...]
        cot[...] = cot_in[...]


def turn_kernel(d, chunk, step, info, labels, pair, w, table, classifier_in, own_in, out, res, own, blocks, cot, *rest):
    scr, (classifier, sems) = dict(zip(SCRATCH, rest)), rest[-2:]

    @pl.when(info[0] == step[0])
    def _():
        fetch = pltpu.make_async_copy(classifier_in, classifier, sems.at[1])
        fetch.start()
        clear_tail(d, scr["cs"])
        res[0] = pair[0]
        res[1] = pair[1]
        copy = pltpu.make_async_copy(res.at[pl.ds(0, 2)], own, sems.at[0])
        copy.start()
        forward_section(d, info[1], w, table, res, out.at[1], scr)
        fetch.wait()
        head(d, out.at[1], labels, chunk * d.n, classifier, scr)
        backward_section(d, info, w, table, res, blocks, cot, scr, out)
        copy.wait()


def send_kernel(d, n_chunks, n_taps, n_steps, depth, info, *refs):
    blocks, refs = refs[:n_chunks], refs[n_chunks:]
    every, cot = refs[: n_chunks * n_steps], refs[n_chunks * n_steps : n_chunks * (n_steps + 1)]
    refs = refs[n_chunks * (n_steps + 1) :]
    outs, (res, tap_blocks, xs, cs, sums) = refs[:depth], refs[depth:]
    slots = 2
    share = outs[0].shape[1]
    place = info[2]
    below = n_chunks * slots * d.flat
    for k in range(depth):
        for chunk in range(n_chunks):
            start = chunk * slots * d.flat
            outs[k][start : start + slots * d.flat, :] = blocks[chunk][k]
    for step in range(n_steps):

        @pl.when(info[0] == step)
        def _():
            for chunk in range(n_chunks):
                res[chunk] = every[chunk * n_steps + step][...]

    for slot in range(slots):
        for branch, width in ((0, 3), (1, 5)):
            first = slot * n_taps + (0 if width == 3 else 9)
            reach = width // 2
            for chunk in range(n_chunks):
                source = res[chunk][slot + 1 - branch]
                xs[...] = jnp.maximum(source.astype(F32), 0.0)
                cs[...] = cot[chunk][2 * slot + branch].astype(F32)
                for tile in range(d.tiles):
                    for row in range(width):
                        for column in range(width):
                            total = None
                            for y in range(d.side):
                                for x in range(d.side):
                                    yy, xx = y + row - reach, x + column - reach
                                    if 0 <= yy < d.side and 0 <= xx < d.side:
                                        v = (
                                            xs[tile, at(yy * d.side + xx), :]
                                            * cs[tile, at(y * d.side + x), :]
                                        )
                                        total = v if total is None else total + v
                            tap = first + row * width + column
                            if chunk == 0:
                                sums[tile, at(tap), :] = total
                            else:
                                sums[tile, at(tap), :] += total
    count = slots * n_taps
    padded = tap_blocks.shape[1]
    sums[:, count * SUB :, :] = jnp.zeros((d.tiles, (padded - count) * SUB, LANE), F32)
    pieces = []
    for part in range(d.parts):
        for tile in range(d.tiles):
            total = None
            for image in range(d.n):
                v = sums[tile, pl.ds(part * d.n + image, padded, stride=SUB), :]
                total = v if total is None else total + v
            pieces.append(total)
    value = jnp.concatenate(pieces, axis=1).astype(BF)
    for other in range(depth):
        tap_blocks[place ^ other] = value[:, other * share : (other + 1) * share]
    for k in range(depth):
        outs[k][below:, :] = tap_blocks[k]


def again_kernel(d, depth, n_chunks, info, w, table, *refs):
    lots = depth * n_chunks
    pairs, (acts, maps, fresh, taps, more, xs, cs, sems) = refs[:lots], refs[lots:]
    copies = [
        pltpu.make_async_copy(pairs[lot], maps.at[lot], sems.at[lot]) for lot in range(lots)
    ]
    for copy in copies:
        copy.start()
    clear_tail(d, cs)
    spread_taps(d, table, 0, taps)
    spread_taps(d, table, 1, more)
    for copy in copies:
        copy.wait()

    def place(lot):
        return pl.ds(pl.multiple_of(lot * d.flat, 16), d.flat)

    @pl.loop(0, lots)
    def _(lot):
        acts[0, place(lot), :] = branch_rows(d, maps[lot, 1], 3, taps, xs, cs)
        acts[1, place(lot), :] = branch_rows(d, maps[lot, 0], 5, taps, xs, cs)

    @pl.when(info[1] > 1)
    def _():
        fresh[...] = jnp.dot(acts[0], w[0, 0], preferred_element_type=F32)
        fresh[...] += jnp.dot(acts[1], w[0, 1], preferred_element_type=F32)

        @pl.loop(0, lots)
        def _(lot):
            acts[3, place(lot), :] = branch_rows(d, maps[lot, 1], 5, more, xs, cs)
            from_rows(d, fresh[place(lot), :], cs)
            value = cs[:, : d.rows, :].astype(BF)
            clear_tail(d, cs)
            acts[2, place(lot), :] = branch_rows(d, value, 3, more, xs, cs)

    @pl.when(info[1] <= 1)
    def _():
        acts[2:4] = jnp.zeros((2,) + acts.shape[1:], BF)


def product_kernel(d, n_chunks, depth, core, *refs):
    acts, blocks, (mine, other) = refs[0], refs[1:-2], refs[-2:]
    share = blocks[0].shape[-1]
    half = share // 2
    below = n_chunks * 2 * d.flat

    def write(low):
        high = half - low
        for slot in range(2):
            dh = [
                blocks[line][(2 * chunk + slot) * d.flat : (2 * chunk + slot + 1) * d.flat, :]
                for line in range(depth)
                for chunk in range(n_chunks)
            ]
            dh = jnp.concatenate(dh, axis=0)
            for branch in range(2):
                grad = lax.dot_general(
                    dh, acts[2 * slot + branch], TN, preferred_element_type=F32
                )
                rows = slice((2 * slot + branch) * half, (2 * slot + branch + 1) * half)
                mine[rows, :] = grad[low : low + half, :]
                other[rows, :] = grad[high : high + half, :].astype(BF)
        total = None
        for line in range(depth):
            v = blocks[line][below:, :].astype(F32)
            total = v if total is None else total + v
        mine[4 * half :, :half] = total[:, low : low + half]
        other[4 * half :, :] = jnp.concatenate(
            [total[:, high : high + half], jnp.zeros((total.shape[0], d.feat - half), F32)], axis=1
        ).astype(BF)

    @pl.when(core[0] == 0)
    def _():
        write(0)

    @pl.when(core[0] != 0)
    def _():
        write(half)


def sum_kernel(d, mine, received, grad, three, five):
    half = grad.shape[2]
    for slot in range(2):
        for branch in range(2):
            rows = slice((2 * slot + branch) * half, (2 * slot + branch + 1) * half)
            grad[slot, branch] = mine[rows, :] + received[rows, :].astype(F32)
    taps = mine[4 * half :, :half] + received[4 * half :, :].astype(F32)[:, :half]
    n_three, n_five = three.shape[0], five.shape[0]
    for slot in range(2):
        first = slot * (n_three + n_five)
        for tap in range(n_three):
            three[tap, slot : slot + 1, :] = taps[first + tap : first + tap + 1, :]
        for tap in range(n_five):
            row = first + n_three + tap
            five[tap, slot : slot + 1, :] = taps[row : row + 1, :]


VM = pl.BlockSpec(memory_space=pltpu.VMEM)
SM = pl.BlockSpec(memory_space=pltpu.SMEM)
ANY = pl.BlockSpec(memory_space=pl.ANY)
PARAMS = pltpu.CompilerParams(vmem_limit_bytes=12 * 1024 * 1024)
SHORT = pl.CostEstimate(flops=10**6, bytes_accessed=10**4, transcendentals=0)
WIDE = pltpu.CompilerParams(vmem_limit_bytes=20 * 1024 * 1024)


def exchange(value, axis, pairs):
    return lax.ppermute(value, axis, pairs)


def neighbour_pairs(size, low):
    if size == 1:
        return [(0, 0)]
    if low % 2 == 0:
        return [(i, i ^ 1) if (i ^ 1) < size else (i, i) for i in range(size)]
    return [(i, (i + 1) % size if i % 2 else (i - 1) % size) for i in range(size)]


CHUNKS = 2


def per_device(stem, labels, cell_count, pointwise, depth_three, depth_five, classifier):
    segments = lax.axis_size("segment")
    replicas = lax.axis_size("dp")
    here = lax.axis_index("segment").astype(jnp.int32)
    replica = lax.axis_index("dp").astype(jnp.int32)
    depth = replicas // 2
    info = jnp.stack([here, cell_count[0], replica // 2])
    core = (replica % 2).reshape(1)
    micro, side, _, feat = stem.shape
    slots = pointwise.shape[0]
    d = Dims(micro // CHUNKS, side, feat)
    n_three, n_five = depth_three.shape[1], depth_five.shape[1]
    n_taps = n_three + n_five
    share = feat // depth
    half = share // 2
    packed = (d.tiles, d.rows, LANE)
    pair_t = jax.ShapeDtypeStruct((2,) + packed, BF)
    res_t = jax.ShapeDtypeStruct((3,) + packed, BF)
    cot_t = jax.ShapeDtypeStruct((4,) + packed, BF)
    blocks_t = jax.ShapeDtypeStruct((depth, slots * d.flat, share), BF)
    scratch = scratch_shapes(d, n_taps)
    stem_t = stem.transpose(1, 2, 0, 3).astype(F32)
    table = jnp.concatenate([depth_three.transpose(1, 0, 2), depth_five.transpose(1, 0, 2)], axis=0)
    weights = (pointwise, table.astype(F32))

    def at_step(step):
        return jnp.full((1,), step, jnp.int32)

    def forward_call(chunk, fresh):
        return jax.jit(
            pl.pallas_call(
                functools.partial(fresh_kernel if fresh else forward_kernel, d, chunk),
                out_shape=(pair_t, res_t, pair_t),
                in_specs=[SM, SM, VM, VM, VM] + [ANY] * (0 if fresh else 1),
                out_specs=(VM, VM, ANY),
                scratch_shapes=scratch + [pltpu.SemaphoreType.DMA((1,))],
                input_output_aliases={} if fresh else {5: 2},
                compiler_params=PARAMS,
                cost_estimate=SHORT,
                name="forward",
            )
        )

    def turn_call(chunk):
        return jax.jit(
            pl.pallas_call(
                functools.partial(turn_kernel, d, chunk),
                out_shape=(pair_t, res_t, pair_t, blocks_t, cot_t),
                in_specs=[SM, SM, SM, VM, VM, VM, ANY, ANY],
                out_specs=(VM, VM, ANY, VM, VM),
                scratch_shapes=scratch
                + [pltpu.VMEM(classifier.shape[::-1], BF), pltpu.SemaphoreType.DMA((2,))],
                input_output_aliases={7: 2},
                compiler_params=PARAMS,
                cost_estimate=SHORT,
                name="turn",
            )
        )

    def backward_body(has_out):
        def body(step, info, g, w, table, res, blocks_in, cot_in, *rest):
            out, rest = (rest[0], rest[1:]) if has_out else (None, rest)
            backward_kernel(d, step, info, g, w, table, res, blocks_in, cot_in, out, *rest)

        return body

    def backward_call(has_out):
        first = 1 if has_out else 0
        return jax.jit(
            pl.pallas_call(
                backward_body(has_out),
                out_shape=((pair_t,) if has_out else ()) + (blocks_t, cot_t),
                in_specs=[SM, SM] + [VM] * 6,
                out_specs=(VM,) * (2 + first),
                scratch_shapes=scratch,
                input_output_aliases={6: first, 7: first + 1},
                compiler_params=PARAMS,
                cost_estimate=SHORT,
                name="backward",
            )
        )

    res = [[] for _ in range(CHUNKS)]
    owns = [None] * CHUNKS
    moving = [None] * CHUNKS
    blocks = [None] * CHUNKS
    cot = [None] * CHUNKS

    forward = forward_call(None, False)
    for step in range(segments - 1):
        for c in range(CHUNKS):
            if step > 0:
                args = (at_step(step), info, moving[c], *weights, owns[c])
                out, kept, owns[c] = forward(*args)
            else:
                args = (at_step(step), info, stem_t, *weights)
                out, kept, owns[c] = forward_call(c, True)(*args)
            res[c].append(kept)
            moving[c] = exchange(out, "segment", neighbour_pairs(segments, step))
    for c in range(CHUNKS):
        out, kept, owns[c], blocks[c], cot[c] = turn_call(c)(
            at_step(segments - 1), info, labels, moving[c], *weights, classifier.T, owns[c]
        )
        res[c].append(kept)
        moving[c] = exchange(out, "segment", neighbour_pairs(segments, segments - 2))

    def along_line(value, k):
        return exchange(value, "dp", [(i, i ^ (2 * k)) for i in range(replicas)])

    gathered = []
    for c in range(CHUNKS):
        own = owns[c]
        if gathered:
            own, gathered[-1] = lax.optimization_barrier((own, gathered[-1]))
        gathered.append([own] + [along_line(own, k) for k in range(1, depth)])

    backward, backward_end = backward_call(True), backward_call(False)
    for step in range(segments - 2, -1, -1):
        for c in range(CHUNKS):
            args = (at_step(step), info, moving[c], *weights, res[c][step], blocks[c], cot[c])
            if step > 0:
                out, blocks[c], cot[c] = backward(*args)
                moving[c] = exchange(out, "segment", neighbour_pairs(segments, step - 1))
            else:
                blocks[c], cot[c] = backward_end(*args)

    tap_rows = -(-slots * n_taps // 16) * 16
    total_rows = CHUNKS * slots * d.flat + tap_rows
    sent = pl.pallas_call(
        functools.partial(send_kernel, d, CHUNKS, n_taps, segments, depth),
        out_shape=(jax.ShapeDtypeStruct((total_rows, share), BF),) * depth,
        in_specs=[SM] + [VM] * (CHUNKS * (segments + 2)),
        out_specs=(VM,) * depth,
        scratch_shapes=[
            pltpu.VMEM((CHUNKS, 3) + packed, BF),
            pltpu.VMEM((depth, tap_rows, share), BF),
            pltpu.VMEM(packed, F32),
            pltpu.VMEM(packed, F32),
            pltpu.VMEM((d.tiles, tap_rows * SUB, LANE), F32),
        ],
        compiler_params=WIDE,
        cost_estimate=SHORT,
        name="send",
    )(info, *blocks, *[r for chunk in res for r in chunk], *cot)
    received = [sent[0]] + [along_line(sent[k], k) for k in range(1, depth)]

    lots = depth * CHUNKS
    acts = pl.pallas_call(
        functools.partial(again_kernel, d, depth, CHUNKS),
        out_shape=jax.ShapeDtypeStruct((4, lots * d.flat, feat), BF),
        in_specs=[SM] + [VM] * 2 + [ANY] * lots,
        out_specs=VM,
        scratch_shapes=[
            pltpu.VMEM((lots, 2) + packed, BF),
            pltpu.VMEM((lots * d.flat, feat), F32),
            scratch[0],
            scratch[0],
            scratch[1],
            scratch[2],
            pltpu.SemaphoreType.DMA((lots,)),
        ],
        compiler_params=WIDE,
        cost_estimate=SHORT,
        name="again",
    )(info, *weights, *[gathered[c][k] for k in range(depth) for c in range(CHUNKS)])
    sum_t = (4 * half + tap_rows, feat)
    mine, other = pl.pallas_call(
        functools.partial(product_kernel, d, CHUNKS, depth),
        out_shape=(jax.ShapeDtypeStruct(sum_t, F32), jax.ShapeDtypeStruct(sum_t, BF)),
        in_specs=[SM] + [VM] * (1 + depth),
        out_specs=(VM, VM),
        compiler_params=WIDE,
        cost_estimate=SHORT,
        name="product",
    )(core, acts, *received)
    swapped = exchange(other, "dp", [(i, i ^ 1) for i in range(replicas)])
    grad, three, five = pl.pallas_call(
        functools.partial(sum_kernel, d),
        out_shape=(
            jax.ShapeDtypeStruct((slots, 2, half, feat), F32),
            jax.ShapeDtypeStruct((n_three, slots, half), F32),
            jax.ShapeDtypeStruct((n_five, slots, half), F32),
        ),
        in_specs=[VM, VM],
        out_specs=(VM,) * 3,
        compiler_params=PARAMS,
        cost_estimate=SHORT,
        name="sum",
    )(mine, swapped)
    return (
        grad.transpose(0, 1, 3, 2),
        three.transpose(1, 0, 2),
        five.transpose(1, 0, 2),
    )


def solution(mesh):
    return jax.shard_map(
        per_device,
        mesh=mesh,
        in_specs=(
            P("dp", None, None, None),
            P("dp"),
            P("segment"),
            P("segment", None, None, None),
            P("segment", None, None),
            P("segment", None, None),
            P(),
        ),
        out_specs=(
            P("segment", None, None, "dp"),
            P("segment", None, "dp"),
            P("segment", None, "dp"),
        ),
        check_vma=False,
    )
```

time: 1010 us -> 87 us (0.09); the launches traced: 995 us -> 86.9 us
  waiting for transfers between devices: 448 us -> 16.5 us
  local copies, waits for them, and re-layouts: 277 us -> 1.61 us
  other arithmetic: 133 us -> 1.9 us
  matrix products: 41.7 us -> 0 us
  starting transfers between devices: 68.8 us -> 44.6 us
  Pallas kernels: 0 us -> 20.8 us
  loops' own time: 12.7 us -> 0 us
  between operations: 14.2 us -> 1.52 us
    ppermute x14 -> x22, waiting for transfers between devices: 336 us -> 16.5 us  [exchange(): return lax.ppermute(value, axis, pairs)]
    another operation x323 -> x0, local copies, waits for them, and re-layouts: 201 us -> none
    psum x2 -> x0, waiting for transfers between devices: 112 us -> none  [the longest x1 67.8 us: per_device(): lax.psum(flat[0].astype(jnp.bfloat16), 'dp').astype(jnp.float32)]
    add x12 -> x0, other arithmetic: 46 us -> none  [pull_back(): return (back_pair, jax.tree.map(lambda a, b: a + b, totals, back_params))]
    dot_general x34 -> x0, matrix products: 41.7 us -> none  [the longest x16 19.9 us: cell(): left = jnp.dot(branch_a.astype(jnp.float32).reshape(-1, feat), weight_pw[0])]
    convert_element_type x24 -> x2, other arithmetic: 36.1 us -> 1.82 us  [the longest x1 0.93 us: per_device(): stem_t = stem.transpose(1, 2, 0, 3).astype(F32)]
    slice x23 -> x0, local copies, waits for them, and re-layouts: 28.2 us -> none  [the longest x16 23.8 us: depthwise(): taps[row * width + column]]
    ppermute x14 -> x22, starting transfers between devices: 68.7 us -> 44.6 us  [exchange(): return lax.ppermute(value, axis, pairs)]
  transfers between devices with their start and end apart: 16 -> 22, of which waited for: 16 -> 6; matrix products, arithmetic and copies ran while one was open for 1% -> 0% of each run, Pallas kernels for 0% -> 17%
where the time goes in v1:
time: 87 us; the launch traced here: 86.9 us
  starting transfers between devices  44.6 us (51%)
  Pallas kernels  20.8 us (24%)
  waiting for transfers between devices  16.5 us (19%)
  other arithmetic  1.9 us (2%)
  local copies, waits for them, and re-layouts  1.61 us (2%)
  between operations  1.52 us (2%)
    ppermute x22, starting transfers between devices, exchange(): return lax.ppermute(value, axis, pairs)  44.6 us
    ppermute x22, waiting for transfers between devices, exchange(): return lax.ppermute(value, axis, pairs)  16.5 us
    pallas_call x1, Pallas kernels, per_device(): pl.pallas_call(functools.partial(again_kernel, d, depth, CHUNKS), out_sha...  4.62 us
    pallas_call x2, Pallas kernels, per_device(): out, kept, owns[c] = forward_call(c, True)(*args)  2.91 us
    pallas_call x4, Pallas kernels, per_device(): out, blocks[c], cot[c] = backward(*args)  2.68 us
    pallas_call x1, Pallas kernels, per_device(): pl.pallas_call(functools.partial(send_kernel, d, CHUNKS, n_taps, segments...  2.52 us
    pallas_call x4, Pallas kernels, per_device(): out, kept, owns[c] = forward(*args)  2.23 us
    pallas_call x2, Pallas kernels, per_device(): blocks[c], cot[c] = backward_end(*args)  2.16 us
  transfers between devices with their start and end apart: 22, of which 6 were waited for; matrix products, arithmetic and copies ran while one was open for 0% of the time, Pallas kernels for 17%

profile of v1, /device:TPU:0, one launch (start us, length us, event | category | flops | bytes accessed | tf_op | source)
XLA Modules:
  0.0 86.9 jit_solution(6050341862302921125)
XLA Ops:
  1.3 0.9 %convert_bitcast_fusion.stem = f32[6,6,4,512]{3,2,1,0:T(4,128)S(1)} fusion(bf16[4,6,6,512]{3,0,2,1:T(4,128)(2,1)} %param.7), kind=kLoop, calls=%fused_computation | loop fusion | flops 73728 | bytes 442368 | tf_op jit(solution)/shard_map/convert_element_type | solution.py:564
  2.2 0.9 %maximum_convert_fusion.table = f32[34,2,512]{2,1,0:T(2,128)S(1)} fusion(bf16[25,2,512]{2,1,0:T(2,128)(2,1)} %bitcast.13, bf16[9,2,512]{2,1,0:T(2,128)(2,1)} %bitcast.14), kind=kLoop, calls=%fused_computation.1 | loop fusion | flops 69632 | bytes 208896 | tf_op jit(solution)/shard_map/convert_element_type | solution.py:566
  3.2 1.6 %copy-done = bf16[2,2,512,512]{3,2,1,0:T(8,128)(2,1)S(1)} copy-done((bf16[2,2,512,512]{3,2,1,0:T(8,128)(2,1)S(1)}, bf16[2,2,512,512]{3,2,1,0:T(8,128)(2,1)}, u32[]{:S(2)}) %copy-start) | copy-done | bytes 2097176
  4.8 1.5 %forward.6 = (bf16[2,1,288,128]{3,2,1,0:T(8,128)(2,1)S(1)}, bf16[3,1,288,128]{3,2,1,0:T(8,128)(2,1)S(1)}, bf16[2,1,288,128]{3,2,1,0:T(8,128)(2,1)S(1)}) custom-call(s32[1]{0:T(128)} %constant.39.clone.1.step, s32[3]{0:T(128)S(1)} %pad_add_fusion.info, f32[6,6,4,512]{3,2,1,0:T(4,128)S(1)} %convert_bitcast_fusion.stem, bf16[2,2,512,512]{3,2,1,0:T(8,128)(2,1)S(1)} %copy-done, ...), custom_call_target="tpu_custom_call" | custom-call | flops 1000000 | bytes 10000 | tf_op jit(solution)/shard_map/jit(wrapped)/forward/pallas_call | solution.py:639
  6.3 2.1 %collective-permute-start = (bf16[2,1,288,128]{3,2,1,0:T(8,128)(2,1)S(1)}, bf16[2,1,288,128]{3,2,1,0:T(8,128)(2,1)S(1)}, u32[]{:S(2)}, u32[]{:S(2)}) collective-permute-start(bf16[2,1,288,128]{3,2,1,0:T(8,128)(2,1)S(1)} %get-tuple-element.61), channel_id=1, source_target_pairs={{0,8},{8,0},{16,24},{24,16},{1,9},{9,1},{17,25},{25,17},{2,10},{10... | collective-permute-start | bytes 442376 | tf_op jit(solution)/shard_map/ppermute | solution.py:529
  8.4 1.5 %forward.9 = (bf16[2,1,288,128]{3,2,1,0:T(8,128)(2,1)S(1)}, bf16[3,1,288,128]{3,2,1,0:T(8,128)(2,1)S(1)}, bf16[2,1,288,128]{3,2,1,0:T(8,128)(2,1)S(1)}) custom-call(s32[1]{0:T(128)} %constant.39.clone.1.step, s32[3]{0:T(128)S(1)} %pad_add_fusion.info, f32[6,6,4,512]{3,2,1,0:T(4,128)S(1)} %convert_bitcast_fusion.stem, bf16[2,2,512,512]{3,2,1,0:T(8,128)(2,1)S(1)} %copy-done, ...), custom_call_target="tpu_custom_call" | custom-call | flops 1000000 | bytes 10000 | tf_op jit(solution)/shard_map/jit(wrapped)/forward/pallas_call | solution.py:639
  9.9 3.1 %collective-permute-done.pair = bf16[2,1,288,128]{3,2,1,0:T(8,128)(2,1)S(1)} collective-permute-done((bf16[2,1,288,128]{3,2,1,0:T(8,128)(2,1)S(1)}, bf16[2,1,288,128]{3,2,1,0:T(8,128)(2,1)S(1)}, u32[]{:S(2)}, u32[]{:S(2)}) %collective-permute-start) | collective-permute-done | bytes 147488 | tf_op jit(solution)/shard_map/ppermute | solution.py:529
  13.6 3.1 %collective-permute-start.1 = (bf16[2,1,288,128]{3,2,1,0:T(8,128)(2,1)S(1)}, bf16[2,1,288,128]{3,2,1,0:T(8,128)(2,1)S(1)}, u32[]{:S(2)}, u32[]{:S(2)}) collective-permute-start(bf16[2,1,288,128]{3,2,1,0:T(8,128)(2,1)S(1)} %get-tuple-element.63), channel_id=1, source_target_pairs={{0,24},{8,16},{16,8},{24,0},{1,25},{9,17},{17,9},{25,1},{2,26},{10... | collective-permute-start | bytes 442376 | tf_op jit(solution)/shard_map/ppermute | solution.py:529
  17.3 1.4 %collective-permute-start.4 = (bf16[2,1,288,128]{3,2,1,0:T(8,128)(2,1)S(1)}, bf16[2,1,288,128]{3,2,1,0:T(8,128)(2,1)S(1)}, u32[]{:S(2)}, u32[]{:S(2)}) collective-permute-start(bf16[2,1,288,128]{3,2,1,0:T(8,128)(2,1)S(1)} %get-tuple-element.70), channel_id=1, source_target_pairs={{0,24},{8,16},{16,8},{24,0},{1,25},{9,17},{17,9},{25,1},{2,26},{10... | collective-permute-start | bytes 442376 | tf_op jit(solution)/shard_map/ppermute | solution.py:529
  18.7 2.2 %collective-permute-done.1.pair = bf16[2,1,288,128]{3,2,1,0:T(8,128)(2,1)S(1)} collective-permute-done((bf16[2,1,288,128]{3,2,1,0:T(8,128)(2,1)S(1)}, bf16[2,1,288,128]{3,2,1,0:T(8,128)(2,1)S(1)}, u32[]{:S(2)}, u32[]{:S(2)}) %collective-permute-start.1) | collective-permute-done | bytes 147488 | tf_op jit(solution)/shard_map/ppermute | solution.py:529
  21.5 4.0 %collective-permute-start.2 = (bf16[2,1,288,128]{3,2,1,0:T(8,128)(2,1)S(1)}, bf16[2,1,288,128]{3,2,1,0:T(8,128)(2,1)S(1)}, u32[]{:S(2)}, u32[]{:S(2)}) collective-permute-start(bf16[2,1,288,128]{3,2,1,0:T(8,128)(2,1)S(1)} %get-tuple-element.65), channel_id=1, source_target_pairs={{0,8},{8,0},{16,24},{24,16},{1,9},{9,1},{17,25},{25,17},{2,10},{10... | collective-permute-start | bytes 442376 | tf_op jit(solution)/shard_map/ppermute | solution.py:529
  26.0 2.6 %collective-permute-start.5 = (bf16[2,1,288,128]{3,2,1,0:T(8,128)(2,1)S(1)}, bf16[2,1,288,128]{3,2,1,0:T(8,128)(2,1)S(1)}, u32[]{:S(2)}, u32[]{:S(2)}) collective-permute-start(bf16[2,1,288,128]{3,2,1,0:T(8,128)(2,1)S(1)} %get-tuple-element.72), channel_id=1, source_target_pairs={{0,8},{8,0},{16,24},{24,16},{1,9},{9,1},{17,25},{25,17},{2,10},{10... | collective-permute-start | bytes 442376 | tf_op jit(solution)/shard_map/ppermute | solution.py:529
  28.6 1.5 %collective-permute-done.2.pair = bf16[2,1,288,128]{3,2,1,0:T(8,128)(2,1)S(1)} collective-permute-done((bf16[2,1,288,128]{3,2,1,0:T(8,128)(2,1)S(1)}, bf16[2,1,288,128]{3,2,1,0:T(8,128)(2,1)S(1)}, u32[]{:S(2)}, u32[]{:S(2)}) %collective-permute-start.2) | collective-permute-done | bytes 147488 | tf_op jit(solution)/shard_map/ppermute | solution.py:529
  30.7 2.1 %collective-permute-start.15 = (bf16[2,1,288,128]{3,2,1,0:T(8,128)(2,1)S(1)}, bf16[2,1,288,128]{3,2,1,0:T(8,128)(2,1)S(1)}, u32[]{:S(2)}, u32[]{:S(2)}) collective-permute-start(bf16[2,1,288,128]{3,2,1,0:T(8,128)(2,1)S(1)} %get-tuple-element.93), channel_id=1, source_target_pairs={{0,8},{8,0},{16,24},{24,16},{1,9},{9,1},{17,25},{25,17},{2,10},{10... | collective-permute-start | bytes 442376 | tf_op jit(solution)/shard_map/ppermute | solution.py:529
  33.6 2.1 %collective-permute-start.12 = (bf16[2,1,288,128]{3,2,1,0:T(8,128)(2,1)S(1)}, bf16[2,1,288,128]{3,2,1,0:T(8,128)(2,1)S(1)}, u32[]{:S(2)}, u32[]{:S(2)}) collective-permute-start(bf16[2,1,288,128]{3,2,1,0:T(8,128)(2,1)S(1)} %get-tuple-element.80), channel_id=1, source_target_pairs={{0,8},{8,0},{16,24},{24,16},{1,9},{9,1},{17,25},{25,17},{2,10},{10... | collective-permute-start | bytes 442376 | tf_op jit(solution)/shard_map/ppermute | solution.py:529
  36.6 6.2 %collective-permute-start.16 = (bf16[2,1,288,128]{3,2,1,0:T(8,128)(2,1)S(1)}, bf16[2,1,288,128]{3,2,1,0:T(8,128)(2,1)S(1)}, u32[]{:S(2)}, u32[]{:S(2)}) collective-permute-start(bf16[2,1,288,128]{3,2,1,0:T(8,128)(2,1)S(1)} %get-tuple-element.97), channel_id=1, source_target_pairs={{0,24},{8,16},{16,8},{24,0},{1,25},{9,17},{17,9},{25,1},{2,26},{10... | collective-permute-start | bytes 442376 | tf_op jit(solution)/shard_map/ppermute | solution.py:529
  43.5 4.1 %collective-permute-start.13 = (bf16[2,1,288,128]{3,2,1,0:T(8,128)(2,1)S(1)}, bf16[2,1,288,128]{3,2,1,0:T(8,128)(2,1)S(1)}, u32[]{:S(2)}, u32[]{:S(2)}) collective-permute-start(bf16[2,1,288,128]{3,2,1,0:T(8,128)(2,1)S(1)} %get-tuple-element.84), channel_id=1, source_target_pairs={{0,24},{8,16},{16,8},{24,0},{1,25},{9,17},{17,9},{25,1},{2,26},{10... | collective-permute-start | bytes 442376 | tf_op jit(solution)/shard_map/ppermute | solution.py:529
  47.6 3.6 %collective-permute-start.8 = (bf16[2,1,288,128]{3,2,1,0:T(8,128)(2,1)S(1)}, bf16[2,1,288,128]{3,2,1,0:T(8,128)(2,1)S(1)}, u32[]{:S(2)}, u32[]{:S(2)}) collective-permute-start(bf16[2,1,288,128]{3,2,1,0:T(8,128)(2,1)S(1)} %get-tuple-element.75.refs_0_), channel_id=1, source_target_pairs={{0,6},{1,7},{2,4},{3,5},{4,2},{5,3},{6,0},{7,1},{8,14},{9,15},{10,... | collective-permute-start | bytes 442376 | tf_op jit(solution)/shard_map/ppermute | solution.py:529
  52.6 1.6 %collective-permute-start.17 = (bf16[2,1,288,128]{3,2,1,0:T(8,128)(2,1)S(1)}, bf16[2,1,288,128]{3,2,1,0:T(8,128)(2,1)S(1)}, u32[]{:S(2)}, u32[]{:S(2)}) collective-permute-start(bf16[2,1,288,128]{3,2,1,0:T(8,128)(2,1)S(1)} %get-tuple-element.101), channel_id=1, source_target_pairs={{0,8},{8,0},{16,24},{24,16},{1,9},{9,1},{17,25},{25,17},{2,10},{10... | collective-permute-start | bytes 442376 | tf_op jit(solution)/shard_map/ppermute | solution.py:529
  55.0 1.9 %collective-permute-start.14 = (bf16[2,1,288,128]{3,2,1,0:T(8,128)(2,1)S(1)}, bf16[2,1,288,128]{3,2,1,0:T(8,128)(2,1)S(1)}, u32[]{:S(2)}, u32[]{:S(2)}) collective-permute-start(bf16[2,1,288,128]{3,2,1,0:T(8,128)(2,1)S(1)} %get-tuple-element.88), channel_id=1, source_target_pairs={{0,8},{8,0},{16,24},{24,16},{1,9},{9,1},{17,25},{25,17},{2,10},{10... | collective-permute-start | bytes 442376 | tf_op jit(solution)/shard_map/ppermute | solution.py:529
  56.8 7.8 %collective-permute-done.7.refs_4_ = bf16[2,1,288,128]{3,2,1,0:T(8,128)(2,1)S(1)} collective-permute-done((bf16[2,1,288,128]{3,2,1,0:T(8,128)(2,1)S(1)}, bf16[2,1,288,128]{3,2,1,0:T(8,128)(2,1)S(1)}, u32[]{:S(2)}, u32[]{:S(2)}) %collective-permute-start.7) | collective-permute-done | bytes 147488 | tf_op jit(solution)/shard_map/ppermute | solution.py:529
  64.6 1.6 %collective-permute-start.11 = (bf16[2,1,288,128]{3,2,1,0:T(8,128)(2,1)S(1)}, bf16[2,1,288,128]{3,2,1,0:T(8,128)(2,1)S(1)}, u32[]{:S(2)}, u32[]{:S(2)}) collective-permute-start(bf16[2,1,288,128]{3,2,1,0:T(8,128)(2,1)S(1)} %get-tuple-element.76.refs_1_), channel_id=1, source_target_pairs={{0,6},{1,7},{2,4},{3,5},{4,2},{5,3},{6,0},{7,1},{8,14},{9,15},{10,... | collective-permute-start | bytes 442376 | tf_op jit(solution)/shard_map/ppermute | solution.py:529
  66.2 2.8 %collective-permute-start.9 = (bf16[2,1,288,128]{3,2,1,0:T(8,128)(2,1)S(1)}, bf16[2,1,288,128]{3,2,1,0:T(8,128)(2,1)}, u32[]{:S(2)}, u32[]{:S(2)}) collective-permute-start(bf16[2,1,288,128]{3,2,1,0:T(8,128)(2,1)S(1)} %get-tuple-element.76.refs_1_), channel_id=1, source_target_pairs={{0,2},{1,3},{2,0},{3,1},{4,6},{5,7},{6,4},{7,5},{8,10},{9,11},{10,... | collective-permute-start | bytes 442376 | tf_op jit(solution)/shard_map/ppermute | solution.py:529
  69.0 1.1 %backward.11 = (bf16[4,160,128]{2,1,0:T(8,128)(2,1)S(1)}, bf16[4,1,288,128]{3,2,1,0:T(8,128)(2,1)S(1)}) custom-call(s32[1]{0:T(128)} %constant.39.clone.1.step, s32[3]{0:T(128)S(1)} %pad_add_fusion.info, bf16[2,1,288,128]{3,2,1,0:T(8,128)(2,1)S(1)} %collective-permute-done.17.g, ...), custom_call_target="tpu_custom_call", output_to_operand_aliasing={{0}: (6, {}), {1}: (7, {})} | custom-call | flops 1000000 | bytes 10000 | tf_op jit(solution)/shard_map/jit(wrapped)/backward/pallas_call | solution.py:667
  70.1 1.1 %backward.8 = (bf16[4,160,128]{2,1,0:T(8,128)(2,1)S(1)}, bf16[4,1,288,128]{3,2,1,0:T(8,128)(2,1)S(1)}) custom-call(s32[1]{0:T(128)} %constant.39.clone.1.step, s32[3]{0:T(128)S(1)} %pad_add_fusion.info, bf16[2,1,288,128]{3,2,1,0:T(8,128)(2,1)S(1)} %collective-permute-done.14.g, ...), custom_call_target="tpu_custom_call", output_to_operand_aliasing={{0}: (6, {}), {1}: (7, {})} | custom-call | flops 1000000 | bytes 10000 | tf_op jit(solution)/shard_map/jit(wrapped)/backward/pallas_call | solution.py:667
  71.2 2.5 %send.1 = (bf16[400,128]{1,0:T(8,128)(2,1)S(1)}, bf16[400,128]{1,0:T(8,128)(2,1)}, bf16[400,128]{1,0:T(8,128)(2,1)}, bf16[400,128]{1,0:T(8,128)(2,1)}) custom-call(s32[3]{0:T(128)S(1)} %pad_add_fusion.info, bf16[4,160,128]{2,1,0:T(8,128)(2,1)S(1)} %get-tuple-element.92.refs_0_, bf16[4,160,128]{2,1,0:T(8,128)(2,1)S(1)} %get-tuple-element.105.refs_1_, ...), custom_call_target="tpu_custom_call" | custom-call | flops 1000000 | bytes 10000 | tf_op jit(solution)/shard_map/send/pallas_call | solution.py:671
  73.7 2.2 %collective-permute-start.19 = (bf16[400,128]{1,0:T(8,128)(2,1)}, bf16[400,128]{1,0:T(8,128)(2,1)S(1)}, u32[]{:S(2)}, u32[]{:S(2)}) collective-permute-start(bf16[400,128]{1,0:T(8,128)(2,1)} %get-tuple-element.112), channel_id=1, source_target_pairs={{0,4},{1,5},{2,6},{3,7},{4,0},{5,1},{6,2},{7,3},{8,12},{9,13},{10,... | collective-permute-start | bytes 307208 | tf_op jit(solution)/shard_map/ppermute | solution.py:529
  75.9 2.2 %collective-permute-start.20 = (bf16[400,128]{1,0:T(8,128)(2,1)}, bf16[400,128]{1,0:T(8,128)(2,1)}, u32[]{:S(2)}, u32[]{:S(2)}) collective-permute-start(bf16[400,128]{1,0:T(8,128)(2,1)} %get-tuple-element.113), channel_id=1, source_target_pairs={{0,6},{1,7},{2,4},{3,5},{4,2},{5,3},{6,0},{7,1},{8,14},{9,15},{10,... | collective-permute-start | bytes 307208 | tf_op jit(solution)/shard_map/ppermute | solution.py:529
  78.1 4.6 %again.1.refs_0_ = bf16[4,640,512]{2,1,0:T(8,128)(2,1)S(1)} custom-call(s32[3]{0:T(128)S(1)} %pad_add_fusion.info, bf16[2,2,512,512]{3,2,1,0:T(8,128)(2,1)S(1)} %copy-done.1, f32[34,2,512]{2,1,0:T(2,128)S(1)} %maximum_convert_fusion.table, bf16[2,1,288,128]{3,2,1,0:T(8,128)(2,1)S(1)} %get-tuple-element.75.refs_0_, ...), custom_call_target="tpu_custom_call" | custom-call | flops 1000000 | bytes 10000 | tf_op jit(solution)/shard_map/again/pallas_call | solution.py:690
  82.8 1.5 %product.1 = (f32[336,512]{1,0:T(8,128)S(1)}, bf16[336,512]{1,0:T(8,128)(2,1)S(1)}) custom-call(s32[1]{0:T(128)} %bitcast.core, bf16[4,640,512]{2,1,0:T(8,128)(2,1)S(1)} %again.1.refs_0_, bf16[400,128]{1,0:T(8,128)(2,1)S(1)} %get-tuple-element.110.refs_1_, bf16[400,128]{1,0:T(8,128)(2,1)S(1)} %collective-permute-done.18.refs_2_, ...), custom_call_target="tpu_custom_call" | custom-call | flops 1000000 | bytes 10000 | tf_op jit(solution)/shard_map/product/pallas_call | solution.py:709
  84.4 1.6 %collective-permute-done.21.received = bf16[336,512]{1,0:T(8,128)(2,1)S(1)} collective-permute-done((bf16[336,512]{1,0:T(8,128)(2,1)S(1)}, bf16[336,512]{1,0:T(8,128)(2,1)S(1)}, u32[]{:S(2)}, u32[]{:S(2)}) %collective-permute-start.21) | collective-permute-done | bytes 344096 | tf_op jit(solution)/shard_map/ppermute | solution.py:529
  86.0 0.9 sum.1
  (41 shorter events, 7.6 us)
Async XLA Ops:
  3.2 1.6 %copy-start = (bf16[2,2,512,512]{3,2,1,0:T(8,128)(2,1)S(1)}, bf16[2,2,512,512]{3,2,1,0:T(8,128)(2,1)}, u32[]{:S(2)}) copy-start(bf16[2,2,512,512]{3,2,1,0:T(8,128)(2,1)} %w.29) | copy-start | bytes 6291460
  4.8 8.2 %copy-start.1 = (bf16[2,2,512,512]{3,2,1,0:T(8,128)(2,1)S(1)}, bf16[2,2,512,512]{3,2,1,0:T(8,128)(2,1)}, u32[]{:S(2)}) copy-start(bf16[2,2,512,512]{3,2,1,0:T(8,128)(2,1)} %w.29) | copy-start | bytes 6291460
  6.3 6.7 %collective-permute-start = (bf16[2,1,288,128]{3,2,1,0:T(8,128)(2,1)S(1)}, bf16[2,1,288,128]{3,2,1,0:T(8,128)(2,1)S(1)}, u32[]{:S(2)}, u32[]{:S(2)}) collective-permute-start(bf16[2,1,288,128]{3,2,1,0:T(8,128)(2,1)S(1)} %get-tuple-element.61), channel_id=1, source_target_pairs={{0,8},{8,0},{16,24},{24,16},{1,9},{9,1},{17,25},{25,17},{2,10},{10... | collective-permute-start | bytes 442376 | tf_op jit(solution)/shard_map/ppermute | solution.py:529
  9.8 6.9 %collective-permute-start.3 = (bf16[2,1,288,128]{3,2,1,0:T(8,128)(2,1)S(1)}, bf16[2,1,288,128]{3,2,1,0:T(8,128)(2,1)S(1)}, u32[]{:S(2)}, u32[]{:S(2)}) collective-permute-start(bf16[2,1,288,128]{3,2,1,0:T(8,128)(2,1)S(1)} %get-tuple-element.68), channel_id=1, source_target_pairs={{0,8},{8,0},{16,24},{24,16},{1,9},{9,1},{17,25},{25,17},{2,10},{10... | collective-permute-start | bytes 442376 | tf_op jit(solution)/shard_map/ppermute | solution.py:529
  13.6 7.3 %collective-permute-start.1 = (bf16[2,1,288,128]{3,2,1,0:T(8,128)(2,1)S(1)}, bf16[2,1,288,128]{3,2,1,0:T(8,128)(2,1)S(1)}, u32[]{:S(2)}, u32[]{:S(2)}) collective-permute-start(bf16[2,1,288,128]{3,2,1,0:T(8,128)(2,1)S(1)} %get-tuple-element.63), channel_id=1, source_target_pairs={{0,24},{8,16},{16,8},{24,0},{1,25},{9,17},{17,9},{25,1},{2,26},{10... | collective-permute-start | bytes 442376 | tf_op jit(solution)/shard_map/ppermute | solution.py:529
  17.3 12.8 %copy-start.2 = (bf16[512,1000]{0,1:T(8,128)(2,1)S(1)}, bf16[512,1000]{0,1:T(8,128)(2,1)}, u32[]{:S(2)}) copy-start(bf16[512,1000]{0,1:T(8,128)(2,1)} %param.13) | copy-start | bytes 3072004
  17.3 12.8 %copy-start.3 = (s32[4]{0:T(128)S(1)}, s32[4]{0:T(128)}, u32[]{:S(2)}) copy-start(s32[4]{0:T(128)} %labels.3) | copy-start | bytes 52
  17.3 8.2 %collective-permute-start.4 = (bf16[2,1,288,128]{3,2,1,0:T(8,128)(2,1)S(1)}, bf16[2,1,288,128]{3,2,1,0:T(8,128)(2,1)S(1)}, u32[]{:S(2)}, u32[]{:S(2)}) collective-permute-start(bf16[2,1,288,128]{3,2,1,0:T(8,128)(2,1)S(1)} %get-tuple-element.70), channel_id=1, source_target_pairs={{0,24},{8,16},{16,8},{24,0},{1,25},{9,17},{17,9},{25,1},{2,26},{10... | collective-permute-start | bytes 442376 | tf_op jit(solution)/shard_map/ppermute | solution.py:529
  21.5 8.6 %collective-permute-start.2 = (bf16[2,1,288,128]{3,2,1,0:T(8,128)(2,1)S(1)}, bf16[2,1,288,128]{3,2,1,0:T(8,128)(2,1)S(1)}, u32[]{:S(2)}, u32[]{:S(2)}) collective-permute-start(bf16[2,1,288,128]{3,2,1,0:T(8,128)(2,1)S(1)} %get-tuple-element.65), channel_id=1, source_target_pairs={{0,8},{8,0},{16,24},{24,16},{1,9},{9,1},{17,25},{25,17},{2,10},{10... | collective-permute-start | bytes 442376 | tf_op jit(solution)/shard_map/ppermute | solution.py:529
  26.0 6.8 %collective-permute-start.5 = (bf16[2,1,288,128]{3,2,1,0:T(8,128)(2,1)S(1)}, bf16[2,1,288,128]{3,2,1,0:T(8,128)(2,1)S(1)}, u32[]{:S(2)}, u32[]{:S(2)}) collective-permute-start(bf16[2,1,288,128]{3,2,1,0:T(8,128)(2,1)S(1)} %get-tuple-element.72), channel_id=1, source_target_pairs={{0,8},{8,0},{16,24},{24,16},{1,9},{9,1},{17,25},{25,17},{2,10},{10... | collective-permute-start | bytes 442376 | tf_op jit(solution)/shard_map/ppermute | solution.py:529
  30.7 5.3 %collective-permute-start.15 = (bf16[2,1,288,128]{3,2,1,0:T(8,128)(2,1)S(1)}, bf16[2,1,288,128]{3,2,1,0:T(8,128)(2,1)S(1)}, u32[]{:S(2)}, u32[]{:S(2)}) collective-permute-start(bf16[2,1,288,128]{3,2,1,0:T(8,128)(2,1)S(1)} %get-tuple-element.93), channel_id=1, source_target_pairs={{0,8},{8,0},{16,24},{24,16},{1,9},{9,1},{17,25},{25,17},{2,10},{10... | collective-permute-start | bytes 442376 | tf_op jit(solution)/shard_map/ppermute | solution.py:529
  33.6 9.3 %collective-permute-start.12 = (bf16[2,1,288,128]{3,2,1,0:T(8,128)(2,1)S(1)}, bf16[2,1,288,128]{3,2,1,0:T(8,128)(2,1)S(1)}, u32[]{:S(2)}, u32[]{:S(2)}) collective-permute-start(bf16[2,1,288,128]{3,2,1,0:T(8,128)(2,1)S(1)} %get-tuple-element.80), channel_id=1, source_target_pairs={{0,8},{8,0},{16,24},{24,16},{1,9},{9,1},{17,25},{25,17},{2,10},{10... | collective-permute-start | bytes 442376 | tf_op jit(solution)/shard_map/ppermute | solution.py:529
  36.6 15.3 %collective-permute-start.16 = (bf16[2,1,288,128]{3,2,1,0:T(8,128)(2,1)S(1)}, bf16[2,1,288,128]{3,2,1,0:T(8,128)(2,1)S(1)}, u32[]{:S(2)}, u32[]{:S(2)}) collective-permute-start(bf16[2,1,288,128]{3,2,1,0:T(8,128)(2,1)S(1)} %get-tuple-element.97), channel_id=1, source_target_pairs={{0,24},{8,16},{16,8},{24,0},{1,25},{9,17},{17,9},{25,1},{2,26},{10... | collective-permute-start | bytes 442376 | tf_op jit(solution)/shard_map/ppermute | solution.py:529
  43.5 10.8 %collective-permute-start.13 = (bf16[2,1,288,128]{3,2,1,0:T(8,128)(2,1)S(1)}, bf16[2,1,288,128]{3,2,1,0:T(8,128)(2,1)S(1)}, u32[]{:S(2)}, u32[]{:S(2)}) collective-permute-start(bf16[2,1,288,128]{3,2,1,0:T(8,128)(2,1)S(1)} %get-tuple-element.84), channel_id=1, source_target_pairs={{0,24},{8,16},{16,8},{24,0},{1,25},{9,17},{17,9},{25,1},{2,26},{10... | collective-permute-start | bytes 442376 | tf_op jit(solution)/shard_map/ppermute | solution.py:529
  47.6 9.3 %collective-permute-start.8 = (bf16[2,1,288,128]{3,2,1,0:T(8,128)(2,1)S(1)}, bf16[2,1,288,128]{3,2,1,0:T(8,128)(2,1)S(1)}, u32[]{:S(2)}, u32[]{:S(2)}) collective-permute-start(bf16[2,1,288,128]{3,2,1,0:T(8,128)(2,1)S(1)} %get-tuple-element.75.refs_0_), channel_id=1, source_target_pairs={{0,6},{1,7},{2,4},{3,5},{4,2},{5,3},{6,0},{7,1},{8,14},{9,15},{10,... | collective-permute-start | bytes 442376 | tf_op jit(solution)/shard_map/ppermute | solution.py:529
  51.2 13.4 %collective-permute-start.7 = (bf16[2,1,288,128]{3,2,1,0:T(8,128)(2,1)S(1)}, bf16[2,1,288,128]{3,2,1,0:T(8,128)(2,1)S(1)}, u32[]{:S(2)}, u32[]{:S(2)}) collective-permute-start(bf16[2,1,288,128]{3,2,1,0:T(8,128)(2,1)S(1)} %get-tuple-element.75.refs_0_), channel_id=1, source_target_pairs={{0,4},{1,5},{2,6},{3,7},{4,0},{5,1},{6,2},{7,3},{8,12},{9,13},{10,... | collective-permute-start | bytes 442376 | tf_op jit(solution)/shard_map/ppermute | solution.py:529
  51.2 13.4 %collective-permute-start.6 = (bf16[2,1,288,128]{3,2,1,0:T(8,128)(2,1)S(1)}, bf16[2,1,288,128]{3,2,1,0:T(8,128)(2,1)S(1)}, u32[]{:S(2)}, u32[]{:S(2)}) collective-permute-start(bf16[2,1,288,128]{3,2,1,0:T(8,128)(2,1)S(1)} %get-tuple-element.75.refs_0_), channel_id=1, source_target_pairs={{0,2},{1,3},{2,0},{3,1},{4,6},{5,7},{6,4},{7,5},{8,10},{9,11},{10,... | collective-permute-start | bytes 442376 | tf_op jit(solution)/shard_map/ppermute | solution.py:529
  52.6 16.4 %collective-permute-start.17 = (bf16[2,1,288,128]{3,2,1,0:T(8,128)(2,1)S(1)}, bf16[2,1,288,128]{3,2,1,0:T(8,128)(2,1)S(1)}, u32[]{:S(2)}, u32[]{:S(2)}) collective-permute-start(bf16[2,1,288,128]{3,2,1,0:T(8,128)(2,1)S(1)} %get-tuple-element.101), channel_id=1, source_target_pairs={{0,8},{8,0},{16,24},{24,16},{1,9},{9,1},{17,25},{25,17},{2,10},{10... | collective-permute-start | bytes 442376 | tf_op jit(solution)/shard_map/ppermute | solution.py:529
  55.0 15.2 %collective-permute-start.14 = (bf16[2,1,288,128]{3,2,1,0:T(8,128)(2,1)S(1)}, bf16[2,1,288,128]{3,2,1,0:T(8,128)(2,1)S(1)}, u32[]{:S(2)}, u32[]{:S(2)}) collective-permute-start(bf16[2,1,288,128]{3,2,1,0:T(8,128)(2,1)S(1)} %get-tuple-element.88), channel_id=1, source_target_pairs={{0,8},{8,0},{16,24},{24,16},{1,9},{9,1},{17,25},{25,17},{2,10},{10... | collective-permute-start | bytes 442376 | tf_op jit(solution)/shard_map/ppermute | solution.py:529
  64.6 11.3 %collective-permute-start.11 = (bf16[2,1,288,128]{3,2,1,0:T(8,128)(2,1)S(1)}, bf16[2,1,288,128]{3,2,1,0:T(8,128)(2,1)S(1)}, u32[]{:S(2)}, u32[]{:S(2)}) collective-permute-start(bf16[2,1,288,128]{3,2,1,0:T(8,128)(2,1)S(1)} %get-tuple-element.76.refs_1_), channel_id=1, source_target_pairs={{0,6},{1,7},{2,4},{3,5},{4,2},{5,3},{6,0},{7,1},{8,14},{9,15},{10,... | collective-permute-start | bytes 442376 | tf_op jit(solution)/shard_map/ppermute | solution.py:529
  66.2 11.9 %collective-permute-start.10 = (bf16[2,1,288,128]{3,2,1,0:T(8,128)(2,1)S(1)}, bf16[2,1,288,128]{3,2,1,0:T(8,128)(2,1)}, u32[]{:S(2)}, u32[]{:S(2)}) collective-permute-start(bf16[2,1,288,128]{3,2,1,0:T(8,128)(2,1)S(1)} %get-tuple-element.76.refs_1_), channel_id=1, source_target_pairs={{0,4},{1,5},{2,6},{3,7},{4,0},{5,1},{6,2},{7,3},{8,12},{9,13},{10,... | collective-permute-start | bytes 442376 | tf_op jit(solution)/shard_map/ppermute | solution.py:529
  66.2 11.9 %collective-permute-start.9 = (bf16[2,1,288,128]{3,2,1,0:T(8,128)(2,1)S(1)}, bf16[2,1,288,128]{3,2,1,0:T(8,128)(2,1)}, u32[]{:S(2)}, u32[]{:S(2)}) collective-permute-start(bf16[2,1,288,128]{3,2,1,0:T(8,128)(2,1)S(1)} %get-tuple-element.76.refs_1_), channel_id=1, source_target_pairs={{0,2},{1,3},{2,0},{3,1},{4,6},{5,7},{6,4},{7,5},{8,10},{9,11},{10,... | collective-permute-start | bytes 442376 | tf_op jit(solution)/shard_map/ppermute | solution.py:529
  73.7 9.0 %collective-permute-start.18 = (bf16[400,128]{1,0:T(8,128)(2,1)}, bf16[400,128]{1,0:T(8,128)(2,1)S(1)}, u32[]{:S(2)}, u32[]{:S(2)}) collective-permute-start(bf16[400,128]{1,0:T(8,128)(2,1)} %get-tuple-element.111), channel_id=1, source_target_pairs={{0,2},{1,3},{2,0},{3,1},{4,6},{5,7},{6,4},{7,5},{8,10},{9,11},{10,... | collective-permute-start | bytes 307208 | tf_op jit(solution)/shard_map/ppermute | solution.py:529
  73.7 9.0 %collective-permute-start.19 = (bf16[400,128]{1,0:T(8,128)(2,1)}, bf16[400,128]{1,0:T(8,128)(2,1)S(1)}, u32[]{:S(2)}, u32[]{:S(2)}) collective-permute-start(bf16[400,128]{1,0:T(8,128)(2,1)} %get-tuple-element.112), channel_id=1, source_target_pairs={{0,4},{1,5},{2,6},{3,7},{4,0},{5,1},{6,2},{7,3},{8,12},{9,13},{10,... | collective-permute-start | bytes 307208 | tf_op jit(solution)/shard_map/ppermute | solution.py:529
  75.9 6.9 %collective-permute-start.20 = (bf16[400,128]{1,0:T(8,128)(2,1)}, bf16[400,128]{1,0:T(8,128)(2,1)}, u32[]{:S(2)}, u32[]{:S(2)}) collective-permute-start(bf16[400,128]{1,0:T(8,128)(2,1)} %get-tuple-element.113), channel_id=1, source_target_pairs={{0,6},{1,7},{2,4},{3,5},{4,2},{5,3},{6,0},{7,1},{8,14},{9,15},{10,... | collective-permute-start | bytes 307208 | tf_op jit(solution)/shard_map/ppermute | solution.py:529
  84.3 1.7 %collective-permute-start.21 = (bf16[336,512]{1,0:T(8,128)(2,1)S(1)}, bf16[336,512]{1,0:T(8,128)(2,1)S(1)}, u32[]{:S(2)}, u32[]{:S(2)}) collective-permute-start(bf16[336,512]{1,0:T(8,128)(2,1)S(1)} %get-tuple-element.115), channel_id=1, source_target_pairs={{0,1},{1,0},{2,3},{3,2},{4,5},{5,4},{6,7},{7,6},{8,9},{9,8},{10,11... | collective-permute-start | bytes 1032200 | tf_op jit(solution)/shard_map/ppermute | solution.py:529

commit v2 on v1

--- a/solution.py
+++ b/solution.py
@@ -45,7 +45,7 @@
 
 
 def spread_taps(d, source, slot, taps_ref):
-    for tap in range(source.shape[0]):
+    for tap in range(source.shape[0] - d.pos):
         value = source[tap, slot : slot + 1]
         for part in range(d.parts):
             for tile in range(d.tiles):
@@ -256,14 +256,13 @@
     g0[...] = jnp.zeros(g0.shape, F32)
 
 
-def load_stem(d, stem, chunk, cs):
-    for y in range(d.side):
-        for x in range(d.side):
-            value = stem[y, x, chunk * d.n : (chunk + 1) * d.n]
-            for part in range(d.parts):
-                for tile in range(d.tiles):
-                    start = (y * d.side + x) * SUB + part * d.n
-                    cs[tile, start : start + d.n, :] = value[:, d.lanes(part, tile)]
+def load_stem(d, n_taps, chunk, table, cs):
+    for position in range(d.pos):
+        value = table[n_taps + position, chunk * d.n : (chunk + 1) * d.n]
+        for part in range(d.parts):
+            for tile in range(d.tiles):
+                start = position * SUB + part * d.n
+                cs[tile, start : start + d.n, :] = value[:, d.lanes(part, tile)]
 
 
 SCRATCH = ("taps", "xs", "cs", "g0", "g1", "g2", "hs")
@@ -292,34 +291,35 @@
         out[0] = res[1]
 
 
-def take_stem(d, chunk, stem, res, scr):
-    load_stem(d, stem, chunk, scr["cs"])
+def take_stem(d, chunk, table, res, scr):
+    load_stem(d, table.shape[0] - d.pos, chunk, table, scr["cs"])
     value = scr["cs"][:, : d.rows, :].astype(BF)
     res[0] = value
     res[1] = value
 
 
-def forward_kernel(d, chunk, step, info, pair, w, table, own_in, out, res, own, *rest):
+def forward_kernel(d, chunk, fresh, step, info, pair, w, table, own_in, out, res, own, *rest):
     sems, scr = rest[-1], dict(zip(SCRATCH, rest))
 
     @pl.when(info[0] == step[0])
     def _():
         count = info[1]
         clear_tail(d, scr["cs"])
-        if own_in is None:
-            take_stem(d, chunk, pair, res, scr)
+        if fresh:
+            take_stem(d, chunk, table, res, scr)
         else:
             res[0] = pair[0]
             res[1] = pair[1]
-        copy = pltpu.make_async_copy(res.at[pl.ds(0, 2)], own, sems.at[0])
+        copy = pltpu.make_async_copy(res.at[pl.ds(0, 2)], own.at[chunk], sems.at[0])
         copy.start()
         forward_section(d, count, w, table, res, out.at[1], scr)
         hand_on(count, res, out)
         copy.wait()
 
 
-def fresh_kernel(d, chunk, step, info, stem, w, table, *rest):
-    forward_kernel(d, chunk, step, info, stem, w, table, None, *rest)
+def fresh_kernel(d, chunk, step, info, w, table, *rest):
+    passed = [None] if chunk == 0 else []
+    forward_kernel(d, chunk, True, step, info, None, w, table, *passed, *rest)
 
 
 def backward_kernel(d, step, info, cotangent, w, table, res, blocks_in, cot_in, out, blocks, cot, *rest):
@@ -347,7 +347,7 @@
         clear_tail(d, scr["cs"])
         res[0] = pair[0]
         res[1] = pair[1]
-        copy = pltpu.make_async_copy(res.at[pl.ds(0, 2)], own, sems.at[0])
+        copy = pltpu.make_async_copy(res.at[pl.ds(0, 2)], own.at[chunk], sems.at[0])
         copy.start()
         forward_section(d, info[1], w, table, res, out.at[1], scr)
         fetch.wait()
@@ -420,14 +420,33 @@
         outs[k][below:, :] = tap_blocks[k]
 
 
-def again_kernel(d, depth, n_chunks, info, w, table, *refs):
+def again_kernel(d, places, depth, n_chunks, counts, where, w, table, *refs):
+    ends, middles, (acts, maps, fresh, taps, more, xs, cs, sems) = (
+        refs[:depth], refs[depth : 2 * depth], refs[2 * depth :]
+    )
     lots = depth * n_chunks
-    pairs, (acts, maps, fresh, taps, more, xs, cs, sems) = refs[:lots], refs[lots:]
-    copies = [
-        pltpu.make_async_copy(pairs[lot], maps.at[lot], sems.at[lot]) for lot in range(lots)
-    ]
-    for copy in copies:
-        copy.start()
+
+    def fetch(sources):
+        return [
+            pltpu.make_async_copy(
+                sources[line], maps.at[pl.ds(line * n_chunks, n_chunks)], sems.at[line]
+            )
+            for line in range(depth)
+        ]
+
+    copies = fetch(ends)
+    at_end = jnp.logical_or(where[0] == 0, where[0] == places - 1)
+
+    @pl.when(at_end)
+    def _():
+        for copy in copies:
+            copy.start()
+
+    @pl.when(jnp.logical_not(at_end))
+    def _():
+        for copy in fetch(middles):
+            copy.start()
+
     clear_tail(d, cs)
     spread_taps(d, table, 0, taps)
     spread_taps(d, table, 1, more)
@@ -442,7 +461,7 @@
         acts[0, place(lot), :] = branch_rows(d, maps[lot, 1], 3, taps, xs, cs)
         acts[1, place(lot), :] = branch_rows(d, maps[lot, 0], 5, taps, xs, cs)
 
-    @pl.when(info[1] > 1)
+    @pl.when(counts[0] > 1)
     def _():
         fresh[...] = jnp.dot(acts[0], w[0, 0], preferred_element_type=F32)
         fresh[...] += jnp.dot(acts[1], w[0, 1], preferred_element_type=F32)
@@ -455,13 +474,14 @@
             clear_tail(d, cs)
             acts[2, place(lot), :] = branch_rows(d, value, 3, more, xs, cs)
 
-    @pl.when(info[1] <= 1)
+    @pl.when(counts[0] <= 1)
     def _():
         acts[2:4] = jnp.zeros((2,) + acts.shape[1:], BF)
 
 
-def product_kernel(d, n_chunks, depth, core, *refs):
-    acts, blocks, (mine, other) = refs[0], refs[1:-2], refs[-2:]
+def product_kernel(d, n_chunks, depth, n_acts, core, *refs):
+    acts, blocks, (mine, other) = refs[:n_acts], refs[n_acts:-2], refs[-2:]
+    each = depth // n_acts
     share = blocks[0].shape[-1]
     half = share // 2
     below = n_chunks * 2 * d.flat
@@ -469,16 +489,21 @@
     def write(low):
         high = half - low
         for slot in range(2):
-            dh = [
-                blocks[line][(2 * chunk + slot) * d.flat : (2 * chunk + slot + 1) * d.flat, :]
-                for line in range(depth)
-                for chunk in range(n_chunks)
-            ]
-            dh = jnp.concatenate(dh, axis=0)
+            dh = []
+            for group in range(n_acts):
+                pieces = [
+                    blocks[line][(2 * chunk + slot) * d.flat : (2 * chunk + slot + 1) * d.flat, :]
+                    for line in range(group * each, (group + 1) * each)
+                    for chunk in range(n_chunks)
+                ]
+                dh.append(jnp.concatenate(pieces, axis=0))
             for branch in range(2):
-                grad = lax.dot_general(
-                    dh, acts[2 * slot + branch], TN, preferred_element_type=F32
-                )
+                grad = None
+                for group in range(n_acts):
+                    v = lax.dot_general(
+                        dh[group], acts[group][2 * slot + branch], TN, preferred_element_type=F32
+                    )
+                    grad = v if grad is None else grad + v
                 rows = slice((2 * slot + branch) * half, (2 * slot + branch + 1) * half)
                 mine[rows, :] = grad[low : low + half, :]
                 other[rows, :] = grad[high : high + half, :].astype(BF)
@@ -520,9 +545,10 @@
 VM = pl.BlockSpec(memory_space=pltpu.VMEM)
 SM = pl.BlockSpec(memory_space=pltpu.SMEM)
 ANY = pl.BlockSpec(memory_space=pl.ANY)
-PARAMS = pltpu.CompilerParams(vmem_limit_bytes=12 * 1024 * 1024)
+PARAMS = pltpu.CompilerParams(vmem_limit_bytes=7 * 1024 * 1024)
 SHORT = pl.CostEstimate(flops=10**6, bytes_accessed=10**4, transcendentals=0)
-WIDE = pltpu.CompilerParams(vmem_limit_bytes=20 * 1024 * 1024)
+LONG_LINE = pltpu.CompilerParams(vmem_limit_bytes=40 * 1024 * 1024)
+WIDE = pltpu.CompilerParams(vmem_limit_bytes=10 * 1024 * 1024)
 
 
 def exchange(value, axis, pairs):
@@ -557,26 +583,41 @@
     half = share // 2
     packed = (d.tiles, d.rows, LANE)
     pair_t = jax.ShapeDtypeStruct((2,) + packed, BF)
+    own_t = jax.ShapeDtypeStruct((CHUNKS, 2) + packed, BF)
     res_t = jax.ShapeDtypeStruct((3,) + packed, BF)
     cot_t = jax.ShapeDtypeStruct((4,) + packed, BF)
     blocks_t = jax.ShapeDtypeStruct((depth, slots * d.flat, share), BF)
     scratch = scratch_shapes(d, n_taps)
-    stem_t = stem.transpose(1, 2, 0, 3).astype(F32)
-    table = jnp.concatenate([depth_three.transpose(1, 0, 2), depth_five.transpose(1, 0, 2)], axis=0)
-    weights = (pointwise, table.astype(F32))
+    wider = ((0, 0), (0, micro - slots), (0, 0))
+    table = jnp.concatenate(
+        [
+            jnp.pad(depth_three.transpose(1, 0, 2), wider),
+            jnp.pad(depth_five.transpose(1, 0, 2), wider),
+            stem.transpose(1, 2, 0, 3).reshape(side * side, micro, feat),
+        ],
+        axis=0,
+    ).astype(F32)
+    weights = (pointwise, table)
 
     def at_step(step):
         return jnp.full((1,), step, jnp.int32)
 
     def forward_call(chunk, fresh):
+        begin = fresh and chunk == 0
+        body = (
+            functools.partial(fresh_kernel, d, chunk)
+            if fresh
+            else functools.partial(forward_kernel, d, chunk, False)
+        )
+        own_at = 4 if fresh else 5
         return jax.jit(
             pl.pallas_call(
-                functools.partial(fresh_kernel if fresh else forward_kernel, d, chunk),
-                out_shape=(pair_t, res_t, pair_t),
-                in_specs=[SM, SM, VM, VM, VM] + [ANY] * (0 if fresh else 1),
+                body,
+                out_shape=(pair_t, res_t, own_t),
+                in_specs=[SM, SM] + [VM] * (own_at - 2) + [ANY] * (0 if begin else 1),
                 out_specs=(VM, VM, ANY),
                 scratch_shapes=scratch + [pltpu.SemaphoreType.DMA((1,))],
-                input_output_aliases={} if fresh else {5: 2},
+                input_output_aliases={} if begin else {own_at: 2},
                 compiler_params=PARAMS,
                 cost_estimate=SHORT,
                 name="forward",
@@ -587,7 +628,7 @@
         return jax.jit(
             pl.pallas_call(
                 functools.partial(turn_kernel, d, chunk),
-                out_shape=(pair_t, res_t, pair_t, blocks_t, cot_t),
+                out_shape=(pair_t, res_t, own_t, blocks_t, cot_t),
                 in_specs=[SM, SM, SM, VM, VM, VM, ANY, ANY],
                 out_specs=(VM, VM, ANY, VM, VM),
                 scratch_shapes=scratch
@@ -623,25 +664,26 @@
         )
 
     res = [[] for _ in range(CHUNKS)]
-    owns = [None] * CHUNKS
+    own = None
     moving = [None] * CHUNKS
     blocks = [None] * CHUNKS
     cot = [None] * CHUNKS
 
-    forward = forward_call(None, False)
+    forward = [forward_call(c, False) for c in range(CHUNKS)]
     for step in range(segments - 1):
         for c in range(CHUNKS):
+            passed = [] if own is None else [own]
             if step > 0:
-                args = (at_step(step), info, moving[c], *weights, owns[c])
-                out, kept, owns[c] = forward(*args)
+                args = (at_step(step), info, moving[c], *weights, *passed)
+                out, kept, own = forward[c](*args)
             else:
-                args = (at_step(step), info, stem_t, *weights)
-                out, kept, owns[c] = forward_call(c, True)(*args)
+                args = (at_step(step), info, *weights, *passed)
+                out, kept, own = forward_call(c, True)(*args)
             res[c].append(kept)
             moving[c] = exchange(out, "segment", neighbour_pairs(segments, step))
     for c in range(CHUNKS):
-        out, kept, owns[c], blocks[c], cot[c] = turn_call(c)(
-            at_step(segments - 1), info, labels, moving[c], *weights, classifier.T, owns[c]
+        out, kept, own, blocks[c], cot[c] = turn_call(c)(
+            at_step(segments - 1), info, labels, moving[c], *weights, classifier.T, own
         )
         res[c].append(kept)
         moving[c] = exchange(out, "segment", neighbour_pairs(segments, segments - 2))
@@ -649,12 +691,40 @@
     def along_line(value, k):
         return exchange(value, "dp", [(i, i ^ (2 * k)) for i in range(replicas)])
 
-    gathered = []
-    for c in range(CHUNKS):
-        own = owns[c]
-        if gathered:
-            own, gathered[-1] = lax.optimization_barrier((own, gathered[-1]))
-        gathered.append([own] + [along_line(own, k) for k in range(1, depth)])
+    def again(ends, middles):
+        lots = len(ends) * CHUNKS
+        return pl.pallas_call(
+            functools.partial(again_kernel, d, depth, len(ends), CHUNKS),
+            out_shape=jax.ShapeDtypeStruct((4, lots * d.flat, feat), BF),
+            in_specs=[SM, SM] + [VM] * 2 + [ANY] * (2 * len(ends)),
+            out_specs=VM,
+            scratch_shapes=[
+                pltpu.VMEM((lots, 2) + packed, BF),
+                pltpu.VMEM((lots * d.flat, feat), F32),
+                scratch[0],
+                scratch[0],
+                scratch[1],
+                scratch[2],
+                pltpu.SemaphoreType.DMA((len(ends),)),
+            ],
+            compiler_params=WIDE if depth <= 4 else LONG_LINE,
+            cost_estimate=SHORT,
+            name="again",
+        )(cell_count, (replica // 2).reshape(1), *weights, *ends, *middles)
+
+    if depth == 4:
+        middle = [(0, 1), (1, 0), (2, 4), (4, 2), (3, 5), (5, 3), (6, 7), (7, 6)]
+        own, moving[0] = lax.optimization_barrier((own, moving[0]))
+        beside = along_line(own, 1)
+        across = exchange(own, "dp", middle)
+        far = along_line(across, 1)
+        across_far = exchange(beside, "dp", middle)
+        outer = [(0, 6), (6, 0), (1, 7), (7, 1), (2, 3), (3, 2), (4, 5), (5, 4)]
+        end_far = exchange(lax.optimization_barrier((own, beside))[0], "dp", outer)
+        acts = [again([own, beside, far, end_far], [own, beside, across_far, across])]
+    else:
+        direct = [along_line(own, k) for k in range(1, depth)]
+        acts = [again([own] + direct, [own] + direct)]
 
     backward, backward_end = backward_call(True), backward_call(False)
     for step in range(segments - 2, -1, -1):
@@ -680,41 +750,22 @@
             pltpu.VMEM(packed, F32),
             pltpu.VMEM((d.tiles, tap_rows * SUB, LANE), F32),
         ],
-        compiler_params=WIDE,
+        compiler_params=WIDE if depth <= 4 else LONG_LINE,
         cost_estimate=SHORT,
         name="send",
     )(info, *blocks, *[r for chunk in res for r in chunk], *cot)
     received = [sent[0]] + [along_line(sent[k], k) for k in range(1, depth)]
 
-    lots = depth * CHUNKS
-    acts = pl.pallas_call(
-        functools.partial(again_kernel, d, depth, CHUNKS),
-        out_shape=jax.ShapeDtypeStruct((4, lots * d.flat, feat), BF),
-        in_specs=[SM] + [VM] * 2 + [ANY] * lots,
-        out_specs=VM,
-        scratch_shapes=[
-            pltpu.VMEM((lots, 2) + packed, BF),
-            pltpu.VMEM((lots * d.flat, feat), F32),
-            scratch[0],
-            scratch[0],
-            scratch[1],
-            scratch[2],
-            pltpu.SemaphoreType.DMA((lots,)),
-        ],
-        compiler_params=WIDE,
-        cost_estimate=SHORT,
-        name="again",
-    )(info, *weights, *[gathered[c][k] for k in range(depth) for c in range(CHUNKS)])
     sum_t = (4 * half + tap_rows, feat)
     mine, other = pl.pallas_call(
-        functools.partial(product_kernel, d, CHUNKS, depth),
+        functools.partial(product_kernel, d, CHUNKS, depth, len(acts)),
         out_shape=(jax.ShapeDtypeStruct(sum_t, F32), jax.ShapeDtypeStruct(sum_t, BF)),
-        in_specs=[SM] + [VM] * (1 + depth),
+        in_specs=[SM] + [VM] * (len(acts) + depth),
         out_specs=(VM, VM),
-        compiler_params=WIDE,
+        compiler_params=WIDE if depth <= 4 else LONG_LINE,
         cost_estimate=SHORT,
         name="product",
-    )(core, acts, *received)
+    )(core, *acts, *received)
     swapped = exchange(other, "dp", [(i, i ^ 1) for i in range(replicas)])
     grad, three, five = pl.pallas_call(
         functools.partial(sum_kernel, d),

time: 87 us -> 84.5 us (0.971); the launches traced: 86.9 us -> 83.4 us
  starting transfers between devices: 44.6 us -> 39.3 us
  local copies, waits for them, and re-layouts: 1.61 us -> 3.92 us
  waiting for transfers between devices: 16.5 us -> 17.8 us
  Pallas kernels: 20.8 us -> 19.8 us
    ppermute x22 -> x21, starting transfers between devices: 44.6 us -> 39.3 us  [exchange(): return lax.ppermute(value, axis, pairs)]
    unnamed x8 -> x16, local copies, waits for them, and re-layouts: 1.61 us -> 3.92 us
    ppermute x22 -> x21, waiting for transfers between devices: 16.5 us -> 17.8 us  [exchange(): return lax.ppermute(value, axis, pairs)]
    pallas_call x8, Pallas kernels: 11.3 us -> 10.2 us  [the longest x1 3.49 us: again(): pl.pallas_call(functools.partial(again_kernel, d, depth, len(ends), CHUNK...]
    convert_element_type x2 -> x1, other arithmetic: 1.82 us -> 1.08 us  [per_device(): table = jnp.concatenate([jnp.pad(depth_three.transpose(1, 0, 2), wider),...]
  transfers between devices with their start and end apart: 22 -> 21, of which waited for: 6 -> 9; matrix products, arithmetic and copies ran while one was open for 0% -> 0% of each run, Pallas kernels for 17% -> 16%
where the time goes in v2:
time: 84.5 us; the launch traced here: 83.4 us
  starting transfers between devices  39.3 us (47%)
  Pallas kernels  19.8 us (23%)
  waiting for transfers between devices  17.8 us (21%)
  local copies, waits for them, and re-layouts  3.92 us (5%)
  between operations  1.48 us (2%)
  other arithmetic  1.16 us (1%)
    ppermute x21, starting transfers between devices, exchange(): return lax.ppermute(value, axis, pairs)  39.3 us
    ppermute x21, waiting for transfers between devices, exchange(): return lax.ppermute(value, axis, pairs)  17.8 us
    unnamed x16, local copies, waits for them, and re-layouts  3.92 us
    pallas_call x1, Pallas kernels, again(): pl.pallas_call(functools.partial(again_kernel, d, depth, len(ends), CHUNK...  3.49 us
    pallas_call x2, Pallas kernels, per_device(): out, kept, own = forward_call(c, True)(*args)  2.91 us
    pallas_call x4, Pallas kernels, per_device(): out, blocks[c], cot[c] = backward(*args)  2.68 us
    pallas_call x1, Pallas kernels, per_device(): pl.pallas_call(functools.partial(send_kernel, d, CHUNKS, n_taps, segments...  2.56 us
    pallas_call x4, Pallas kernels, per_device(): out, kept, own = forward[c](*args)  2.23 us
  transfers between devices with their start and end apart: 21, of which 9 were waited for; matrix products, arithmetic and copies ran while one was open for 0% of the time, Pallas kernels for 16%

profile of v2, /device:TPU:0, one launch (start us, length us, event | category | flops | bytes accessed | tf_op | source)
XLA Modules:
  0.0 83.4 jit_solution(10392065702021329986)
XLA Ops:
  1.4 1.1 %fusion.5.table = f32[70,4,512]{2,1,0:T(4,128)S(1)} fusion(bf16[25,2,512]{2,1,0:T(2,128)(2,1)} %bitcast.15, bf16[9,2,512]{2,1,0:T(2,128)(2,1)} %bitcast.16, bf16[36,4,512]{2,1,0:T(4,128)(2,1)} %bitcast.14), kind=kLoop, calls=%fused_computation.8 | loop fusion | flops 1720320 | bytes 790528 | tf_op jit(solution)/shard_map/convert_element_type | solution.py:599
  2.5 1.6 %copy-done = bf16[2,2,512,512]{3,2,1,0:T(8,128)(2,1)S(1)} copy-done((bf16[2,2,512,512]{3,2,1,0:T(8,128)(2,1)S(1)}, bf16[2,2,512,512]{3,2,1,0:T(8,128)(2,1)}, u32[]{:S(2)}) %copy-start) | copy-done | bytes 2097176
  4.1 1.5 %forward.6 = (bf16[2,1,288,128]{3,2,1,0:T(8,128)(2,1)S(1)}, bf16[3,1,288,128]{3,2,1,0:T(8,128)(2,1)S(1)}, bf16[2,2,1,288,128]{4,3,2,1,0:T(8,128)(2,1)S(1)}) custom-call(s32[1]{0:T(128)} %constant.44.clone.1.step, s32[3]{0:T(128)S(1)} %pad_add_fusion.info, bf16[2,2,512,512]{3,2,1,0:T(8,128)(2,1)S(1)} %copy-done, f32[70,4,512]{2,1,0:T(4,128)S(1)} %fusion.5.table), custom_call_target="tpu_custom_call" | custom-call | flops 1000000 | bytes 10000 | tf_op jit(solution)/shard_map/jit(wrapped)/forward/pallas_call | solution.py:681
  5.5 2.1 %collective-permute-start.1 = (bf16[2,1,288,128]{3,2,1,0:T(8,128)(2,1)S(1)}, bf16[2,1,288,128]{3,2,1,0:T(8,128)(2,1)S(1)}, u32[]{:S(2)}, u32[]{:S(2)}) collective-permute-start(bf16[2,1,288,128]{3,2,1,0:T(8,128)(2,1)S(1)} %get-tuple-element.61), channel_id=1, source_target_pairs={{0,8},{8,0},{16,24},{24,16},{1,9},{9,1},{17,25},{25,17},{2,10},{10... | collective-permute-start | bytes 442376 | tf_op jit(solution)/shard_map/ppermute | solution.py:555
  7.6 1.5 %forward.7 = (bf16[2,1,288,128]{3,2,1,0:T(8,128)(2,1)S(1)}, bf16[3,1,288,128]{3,2,1,0:T(8,128)(2,1)S(1)}, bf16[2,2,1,288,128]{4,3,2,1,0:T(8,128)(2,1)S(1)}) custom-call(s32[1]{0:T(128)} %constant.44.clone.1.step, s32[3]{0:T(128)S(1)} %pad_add_fusion.info, bf16[2,2,512,512]{3,2,1,0:T(8,128)(2,1)S(1)} %copy-done, ...), custom_call_target="tpu_custom_call", output_to_operand_aliasing={{2}: (4, {})} | custom-call | flops 1000000 | bytes 10000 | tf_op jit(solution)/shard_map/jit(wrapped)/forward/pallas_call | solution.py:681
  9.2 3.1 %collective-permute-done.1.pair = bf16[2,1,288,128]{3,2,1,0:T(8,128)(2,1)S(1)} collective-permute-done((bf16[2,1,288,128]{3,2,1,0:T(8,128)(2,1)S(1)}, bf16[2,1,288,128]{3,2,1,0:T(8,128)(2,1)S(1)}, u32[]{:S(2)}, u32[]{:S(2)}) %collective-permute-start.1) | collective-permute-done | bytes 147488 | tf_op jit(solution)/shard_map/ppermute | solution.py:555
  12.8 3.1 %collective-permute-start.3 = (bf16[2,1,288,128]{3,2,1,0:T(8,128)(2,1)S(1)}, bf16[2,1,288,128]{3,2,1,0:T(8,128)(2,1)S(1)}, u32[]{:S(2)}, u32[]{:S(2)}) collective-permute-start(bf16[2,1,288,128]{3,2,1,0:T(8,128)(2,1)S(1)} %get-tuple-element.65), channel_id=1, source_target_pairs={{0,24},{8,16},{16,8},{24,0},{1,25},{9,17},{17,9},{25,1},{2,26},{10... | collective-permute-start | bytes 442376 | tf_op jit(solution)/shard_map/ppermute | solution.py:555
  16.5 1.5 %collective-permute-start.2 = (bf16[2,1,288,128]{3,2,1,0:T(8,128)(2,1)S(1)}, bf16[2,1,288,128]{3,2,1,0:T(8,128)(2,1)S(1)}, u32[]{:S(2)}, u32[]{:S(2)}) collective-permute-start(bf16[2,1,288,128]{3,2,1,0:T(8,128)(2,1)S(1)} %get-tuple-element.64), channel_id=1, source_target_pairs={{0,24},{8,16},{16,8},{24,0},{1,25},{9,17},{17,9},{25,1},{2,26},{10... | collective-permute-start | bytes 442376 | tf_op jit(solution)/shard_map/ppermute | solution.py:555
  18.1 2.1 %collective-permute-done.3.pair = bf16[2,1,288,128]{3,2,1,0:T(8,128)(2,1)S(1)} collective-permute-done((bf16[2,1,288,128]{3,2,1,0:T(8,128)(2,1)S(1)}, bf16[2,1,288,128]{3,2,1,0:T(8,128)(2,1)S(1)}, u32[]{:S(2)}, u32[]{:S(2)}) %collective-permute-start.3) | collective-permute-done | bytes 147488 | tf_op jit(solution)/shard_map/ppermute | solution.py:555
  20.7 3.3 %collective-permute-start.5 = (bf16[2,1,288,128]{3,2,1,0:T(8,128)(2,1)S(1)}, bf16[2,1,288,128]{3,2,1,0:T(8,128)(2,1)S(1)}, u32[]{:S(2)}, u32[]{:S(2)}) collective-permute-start(bf16[2,1,288,128]{3,2,1,0:T(8,128)(2,1)S(1)} %get-tuple-element.69), channel_id=1, source_target_pairs={{0,8},{8,0},{16,24},{24,16},{1,9},{9,1},{17,25},{25,17},{2,10},{10... | collective-permute-start | bytes 442376 | tf_op jit(solution)/shard_map/ppermute | solution.py:555
  24.7 2.6 %collective-permute-start.4 = (bf16[2,1,288,128]{3,2,1,0:T(8,128)(2,1)S(1)}, bf16[2,1,288,128]{3,2,1,0:T(8,128)(2,1)S(1)}, u32[]{:S(2)}, u32[]{:S(2)}) collective-permute-start(bf16[2,1,288,128]{3,2,1,0:T(8,128)(2,1)S(1)} %get-tuple-element.68), channel_id=1, source_target_pairs={{0,8},{8,0},{16,24},{24,16},{1,9},{9,1},{17,25},{25,17},{2,10},{10... | collective-permute-start | bytes 442376 | tf_op jit(solution)/shard_map/ppermute | solution.py:555
  27.2 1.5 %collective-permute-done.5.pair = bf16[2,1,288,128]{3,2,1,0:T(8,128)(2,1)S(1)} collective-permute-done((bf16[2,1,288,128]{3,2,1,0:T(8,128)(2,1)S(1)}, bf16[2,1,288,128]{3,2,1,0:T(8,128)(2,1)S(1)}, u32[]{:S(2)}, u32[]{:S(2)}) %collective-permute-start.5) | collective-permute-done | bytes 147488 | tf_op jit(solution)/shard_map/ppermute | solution.py:555
  29.3 2.0 %collective-permute-start.6 = (bf16[2,1,288,128]{3,2,1,0:T(8,128)(2,1)S(1)}, bf16[2,1,288,128]{3,2,1,0:T(8,128)(2,1)S(1)}, u32[]{:S(2)}, u32[]{:S(2)}) collective-permute-start(bf16[2,1,288,128]{3,2,1,0:T(8,128)(2,1)S(1)} %get-tuple-element.73), channel_id=1, source_target_pairs={{0,8},{8,0},{16,24},{24,16},{1,9},{9,1},{17,25},{25,17},{2,10},{10... | collective-permute-start | bytes 442376 | tf_op jit(solution)/shard_map/ppermute | solution.py:555
  32.1 2.4 %collective-permute-done.6.g = bf16[2,1,288,128]{3,2,1,0:T(8,128)(2,1)S(1)} collective-permute-done((bf16[2,1,288,128]{3,2,1,0:T(8,128)(2,1)S(1)}, bf16[2,1,288,128]{3,2,1,0:T(8,128)(2,1)S(1)}, u32[]{:S(2)}, u32[]{:S(2)}) %collective-permute-start.6) | collective-permute-done | bytes 147488 | tf_op jit(solution)/shard_map/ppermute | solution.py:555
  34.5 3.7 %collective-permute-start.7 = (bf16[2,2,1,288,128]{4,3,2,1,0:T(8,128)(2,1)S(1)}, bf16[2,2,1,288,128]{4,3,2,1,0:T(8,128)(2,1)S(1)}, u32[]{:S(2)}, u32[]{:S(2)}) collective-permute-start(bf16[2,2,1,288,128]{4,3,2,1,0:T(8,128)(2,1)S(1)} %get-tuple-element.75.refs_0_.refs_4_), channel_id=1, source_target_pairs={{0,2},{1,3},{2,0},{3,1},{4,6},{5,7},{6,4},{7,5},{8,10},{9,11},{10,... | collective-permute-start | bytes 884744 | tf_op jit(solution)/shard_map/ppermute | solution.py:555
  38.2 1.4 %collective-permute-start.14 = (bf16[2,1,288,128]{3,2,1,0:T(8,128)(2,1)S(1)}, bf16[2,1,288,128]{3,2,1,0:T(8,128)(2,1)S(1)}, u32[]{:S(2)}, u32[]{:S(2)}) collective-permute-start(bf16[2,1,288,128]{3,2,1,0:T(8,128)(2,1)S(1)} %get-tuple-element.89), channel_id=1, source_target_pairs={{0,8},{8,0},{16,24},{24,16},{1,9},{9,1},{17,25},{25,17},{2,10},{10... | collective-permute-start | bytes 442376 | tf_op jit(solution)/shard_map/ppermute | solution.py:555
  40.3 3.7 %collective-permute-start.12 = (bf16[2,1,288,128]{3,2,1,0:T(8,128)(2,1)S(1)}, bf16[2,1,288,128]{3,2,1,0:T(8,128)(2,1)S(1)}, u32[]{:S(2)}, u32[]{:S(2)}) collective-permute-start(bf16[2,1,288,128]{3,2,1,0:T(8,128)(2,1)S(1)} %get-tuple-element.80), channel_id=1, source_target_pairs={{0,24},{8,16},{16,8},{24,0},{1,25},{9,17},{17,9},{25,1},{2,26},{10... | collective-permute-start | bytes 442376 | tf_op jit(solution)/shard_map/ppermute | solution.py:555
  44.6 4.5 %collective-permute-start.15 = (bf16[2,1,288,128]{3,2,1,0:T(8,128)(2,1)S(1)}, bf16[2,1,288,128]{3,2,1,0:T(8,128)(2,1)S(1)}, u32[]{:S(2)}, u32[]{:S(2)}) collective-permute-start(bf16[2,1,288,128]{3,2,1,0:T(8,128)(2,1)S(1)} %get-tuple-element.93), channel_id=1, source_target_pairs={{0,24},{8,16},{16,8},{24,0},{1,25},{9,17},{17,9},{25,1},{2,26},{10... | collective-permute-start | bytes 442376 | tf_op jit(solution)/shard_map/ppermute | solution.py:555
  49.2 1.3 %collective-permute-start.9 = (bf16[2,2,1,288,128]{4,3,2,1,0:T(8,128)(2,1)S(1)}, bf16[2,2,1,288,128]{4,3,2,1,0:T(8,128)(2,1)S(1)}, u32[]{:S(2)}, u32[]{:S(2)}) collective-permute-start(bf16[2,2,1,288,128]{4,3,2,1,0:T(8,128)(2,1)S(1)} %collective-permute-done.8.refs_7_), channel_id=1, source_target_pairs={{0,2},{1,3},{2,0},{3,1},{4,6},{5,7},{6,4},{7,5},{8,10},{9,11},{10,... | collective-permute-start | bytes 884744 | tf_op jit(solution)/shard_map/ppermute | solution.py:555
  50.5 2.7 %collective-permute-start.10 = (bf16[2,2,1,288,128]{4,3,2,1,0:T(8,128)(2,1)S(1)}, bf16[2,2,1,288,128]{4,3,2,1,0:T(8,128)(2,1)}, u32[]{:S(2)}, u32[]{:S(2)}) collective-permute-start(bf16[2,2,1,288,128]{4,3,2,1,0:T(8,128)(2,1)S(1)} %get-tuple-element.75.refs_0_.refs_4_), channel_id=1, source_target_pairs={{0,6},{6,0},{1,7},{7,1},{2,3},{3,2},{4,5},{5,4},{8,14},{14,8},{9,1... | collective-permute-start | bytes 884744 | tf_op jit(solution)/shard_map/ppermute | solution.py:555
  53.8 2.1 %collective-permute-start.13 = (bf16[2,1,288,128]{3,2,1,0:T(8,128)(2,1)S(1)}, bf16[2,1,288,128]{3,2,1,0:T(8,128)(2,1)S(1)}, u32[]{:S(2)}, u32[]{:S(2)}) collective-permute-start(bf16[2,1,288,128]{3,2,1,0:T(8,128)(2,1)S(1)} %get-tuple-element.84), channel_id=1, source_target_pairs={{0,8},{8,0},{16,24},{24,16},{1,9},{9,1},{17,25},{25,17},{2,10},{10... | collective-permute-start | bytes 442376 | tf_op jit(solution)/shard_map/ppermute | solution.py:555
  57.3 3.3 %collective-permute-done.13.g = bf16[2,1,288,128]{3,2,1,0:T(8,128)(2,1)S(1)} collective-permute-done((bf16[2,1,288,128]{3,2,1,0:T(8,128)(2,1)S(1)}, bf16[2,1,288,128]{3,2,1,0:T(8,128)(2,1)S(1)}, u32[]{:S(2)}, u32[]{:S(2)}) %collective-permute-start.13) | collective-permute-done | bytes 147488 | tf_op jit(solution)/shard_map/ppermute | solution.py:555
  60.6 1.1 %backward.8 = (bf16[4,160,128]{2,1,0:T(8,128)(2,1)S(1)}, bf16[4,1,288,128]{3,2,1,0:T(8,128)(2,1)S(1)}) custom-call(s32[1]{0:T(128)} %constant.44.clone.1.step, s32[3]{0:T(128)S(1)} %pad_add_fusion.info, bf16[2,1,288,128]{3,2,1,0:T(8,128)(2,1)S(1)} %collective-permute-done.13.g, ...), custom_call_target="tpu_custom_call", output_to_operand_aliasing={{0}: (6, {}), {1}: (7, {})} | custom-call | flops 1000000 | bytes 10000 | tf_op jit(solution)/shard_map/jit(wrapped)/backward/pallas_call | solution.py:737
  61.7 1.9 %collective-permute-done.16.g = bf16[2,1,288,128]{3,2,1,0:T(8,128)(2,1)S(1)} collective-permute-done((bf16[2,1,288,128]{3,2,1,0:T(8,128)(2,1)S(1)}, bf16[2,1,288,128]{3,2,1,0:T(8,128)(2,1)S(1)}, u32[]{:S(2)}, u32[]{:S(2)}) %collective-permute-start.16) | collective-permute-done | bytes 147488 | tf_op jit(solution)/shard_map/ppermute | solution.py:555
  63.6 1.1 %backward.11 = (bf16[4,160,128]{2,1,0:T(8,128)(2,1)S(1)}, bf16[4,1,288,128]{3,2,1,0:T(8,128)(2,1)S(1)}) custom-call(s32[1]{0:T(128)} %constant.44.clone.1.step, s32[3]{0:T(128)S(1)} %pad_add_fusion.info, bf16[2,1,288,128]{3,2,1,0:T(8,128)(2,1)S(1)} %collective-permute-done.16.g, ...), custom_call_target="tpu_custom_call", output_to_operand_aliasing={{0}: (6, {}), {1}: (7, {})} | custom-call | flops 1000000 | bytes 10000 | tf_op jit(solution)/shard_map/jit(wrapped)/backward/pallas_call | solution.py:737
  64.7 2.6 %send.1 = (bf16[400,128]{1,0:T(8,128)(2,1)S(1)}, bf16[400,128]{1,0:T(8,128)(2,1)}, bf16[400,128]{1,0:T(8,128)(2,1)}, bf16[400,128]{1,0:T(8,128)(2,1)}) custom-call(s32[3]{0:T(128)S(1)} %pad_add_fusion.info, bf16[4,160,128]{2,1,0:T(8,128)(2,1)S(1)} %get-tuple-element.88.refs_0_, bf16[4,160,128]{2,1,0:T(8,128)(2,1)S(1)} %get-tuple-element.101.refs_1_, ...), custom_call_target="tpu_custom_call" | custom-call | flops 1000000 | bytes 10000 | tf_op jit(solution)/shard_map/send/pallas_call | solution.py:741
  67.9 2.0 %collective-permute-start.18 = (bf16[400,128]{1,0:T(8,128)(2,1)}, bf16[400,128]{1,0:T(8,128)(2,1)}, u32[]{:S(2)}, u32[]{:S(2)}) collective-permute-start(bf16[400,128]{1,0:T(8,128)(2,1)} %get-tuple-element.108), channel_id=1, source_target_pairs={{0,4},{1,5},{2,6},{3,7},{4,0},{5,1},{6,2},{7,3},{8,12},{9,13},{10,... | collective-permute-start | bytes 307208 | tf_op jit(solution)/shard_map/ppermute | solution.py:555
  70.5 2.4 %collective-permute-start.19 = (bf16[400,128]{1,0:T(8,128)(2,1)}, bf16[400,128]{1,0:T(8,128)(2,1)}, u32[]{:S(2)}, u32[]{:S(2)}) collective-permute-start(bf16[400,128]{1,0:T(8,128)(2,1)} %get-tuple-element.109), channel_id=1, source_target_pairs={{0,6},{1,7},{2,4},{3,5},{4,2},{5,3},{6,0},{7,1},{8,14},{9,15},{10,... | collective-permute-start | bytes 307208 | tf_op jit(solution)/shard_map/ppermute | solution.py:555
  73.9 3.5 %again.1.refs_0_ = bf16[4,640,512]{2,1,0:T(8,128)(2,1)S(1)} custom-call(s32[1]{0:T(128)S(6)} %copy.48.counts, s32[1]{0:T(128)} %bitcast.1.where, bf16[2,2,512,512]{3,2,1,0:T(8,128)(2,1)S(1)} %copy-done.1, f32[70,4,512]{2,1,0:T(4,128)S(1)} %fusion.5.table, bf16[2,2,1,288,128]{4,3,2,1,0:T(8,128)(2,1)S(1)} %get-tuple-element.75.refs_0_.refs_4_, ...), custom_call_target="tpu_custom_call" | custom-call | flops 1000000 | bytes 10000 | tf_op jit(solution)/shard_map/again/pallas_call | solution.py:696
  77.5 1.8 %collective-permute-done.18.refs_3_ = bf16[400,128]{1,0:T(8,128)(2,1)} collective-permute-done((bf16[400,128]{1,0:T(8,128)(2,1)}, bf16[400,128]{1,0:T(8,128)(2,1)}, u32[]{:S(2)}, u32[]{:S(2)}) %collective-permute-start.18) | collective-permute-done | bytes 102432 | tf_op jit(solution)/shard_map/ppermute | solution.py:555
  79.3 1.6 %product.1 = (f32[336,512]{1,0:T(8,128)S(1)}, bf16[336,512]{1,0:T(8,128)(2,1)S(1)}) custom-call(s32[1]{0:T(128)} %bitcast.core, bf16[4,640,512]{2,1,0:T(8,128)(2,1)S(1)} %again.1.refs_0_, bf16[400,128]{1,0:T(8,128)(2,1)S(1)} %copy-done.6, bf16[400,128]{1,0:T(8,128)(2,1)} %collective-permute-done.17.refs_2_, ...), custom_call_target="tpu_custom_call" | custom-call | flops 1000000 | bytes 10000 | tf_op jit(solution)/shard_map/product/pallas_call | solution.py:760
  80.9 1.6 %collective-permute-done.20.received = bf16[336,512]{1,0:T(8,128)(2,1)S(1)} collective-permute-done((bf16[336,512]{1,0:T(8,128)(2,1)S(1)}, bf16[336,512]{1,0:T(8,128)(2,1)S(1)}, u32[]{:S(2)}, u32[]{:S(2)}) %collective-permute-start.20) | collective-permute-done | bytes 344096 | tf_op jit(solution)/shard_map/ppermute | solution.py:555
  (46 shorter events, 10.5 us)
Async XLA Ops:
  2.5 1.6 %copy-start = (bf16[2,2,512,512]{3,2,1,0:T(8,128)(2,1)S(1)}, bf16[2,2,512,512]{3,2,1,0:T(8,128)(2,1)}, u32[]{:S(2)}) copy-start(bf16[2,2,512,512]{3,2,1,0:T(8,128)(2,1)} %w.29) | copy-start | bytes 6291460
  4.0 8.2 %copy-start.1 = (bf16[2,2,512,512]{3,2,1,0:T(8,128)(2,1)S(1)}, bf16[2,2,512,512]{3,2,1,0:T(8,128)(2,1)}, u32[]{:S(2)}) copy-start(bf16[2,2,512,512]{3,2,1,0:T(8,128)(2,1)} %w.29) | copy-start | bytes 6291460
  5.5 6.7 %collective-permute-start.1 = (bf16[2,1,288,128]{3,2,1,0:T(8,128)(2,1)S(1)}, bf16[2,1,288,128]{3,2,1,0:T(8,128)(2,1)S(1)}, u32[]{:S(2)}, u32[]{:S(2)}) collective-permute-start(bf16[2,1,288,128]{3,2,1,0:T(8,128)(2,1)S(1)} %get-tuple-element.61), channel_id=1, source_target_pairs={{0,8},{8,0},{16,24},{24,16},{1,9},{9,1},{17,25},{25,17},{2,10},{10... | collective-permute-start | bytes 442376 | tf_op jit(solution)/shard_map/ppermute | solution.py:555
  9.1 6.9 %collective-permute-start = (bf16[2,1,288,128]{3,2,1,0:T(8,128)(2,1)S(1)}, bf16[2,1,288,128]{3,2,1,0:T(8,128)(2,1)S(1)}, u32[]{:S(2)}, u32[]{:S(2)}) collective-permute-start(bf16[2,1,288,128]{3,2,1,0:T(8,128)(2,1)S(1)} %get-tuple-element.60), channel_id=1, source_target_pairs={{0,8},{8,0},{16,24},{24,16},{1,9},{9,1},{17,25},{25,17},{2,10},{10... | collective-permute-start | bytes 442376 | tf_op jit(solution)/shard_map/ppermute | solution.py:555
  12.8 7.4 %collective-permute-start.3 = (bf16[2,1,288,128]{3,2,1,0:T(8,128)(2,1)S(1)}, bf16[2,1,288,128]{3,2,1,0:T(8,128)(2,1)S(1)}, u32[]{:S(2)}, u32[]{:S(2)}) collective-permute-start(bf16[2,1,288,128]{3,2,1,0:T(8,128)(2,1)S(1)} %get-tuple-element.65), channel_id=1, source_target_pairs={{0,24},{8,16},{16,8},{24,0},{1,25},{9,17},{17,9},{25,1},{2,26},{10... | collective-permute-start | bytes 442376 | tf_op jit(solution)/shard_map/ppermute | solution.py:555
  16.5 7.6 %collective-permute-start.2 = (bf16[2,1,288,128]{3,2,1,0:T(8,128)(2,1)S(1)}, bf16[2,1,288,128]{3,2,1,0:T(8,128)(2,1)S(1)}, u32[]{:S(2)}, u32[]{:S(2)}) collective-permute-start(bf16[2,1,288,128]{3,2,1,0:T(8,128)(2,1)S(1)} %get-tuple-element.64), channel_id=1, source_target_pairs={{0,24},{8,16},{16,8},{24,0},{1,25},{9,17},{17,9},{25,1},{2,26},{10... | collective-permute-start | bytes 442376 | tf_op jit(solution)/shard_map/ppermute | solution.py:555
  20.2 8.6 %copy-start.2 = (bf16[512,1000]{0,1:T(8,128)(2,1)S(1)}, bf16[512,1000]{0,1:T(8,128)(2,1)}, u32[]{:S(2)}) copy-start(bf16[512,1000]{0,1:T(8,128)(2,1)} %param.13) | copy-start | bytes 3072004
  20.2 8.6 %copy-start.7 = (s32[4]{0:T(128)S(1)}, s32[4]{0:T(128)}, u32[]{:S(2)}) copy-start(s32[4]{0:T(128)} %labels.3) | copy-start | bytes 52
  20.7 8.0 %collective-permute-start.5 = (bf16[2,1,288,128]{3,2,1,0:T(8,128)(2,1)S(1)}, bf16[2,1,288,128]{3,2,1,0:T(8,128)(2,1)S(1)}, u32[]{:S(2)}, u32[]{:S(2)}) collective-permute-start(bf16[2,1,288,128]{3,2,1,0:T(8,128)(2,1)S(1)} %get-tuple-element.69), channel_id=1, source_target_pairs={{0,8},{8,0},{16,24},{24,16},{1,9},{9,1},{17,25},{25,17},{2,10},{10... | collective-permute-start | bytes 442376 | tf_op jit(solution)/shard_map/ppermute | solution.py:555
  24.7 6.7 %collective-permute-start.4 = (bf16[2,1,288,128]{3,2,1,0:T(8,128)(2,1)S(1)}, bf16[2,1,288,128]{3,2,1,0:T(8,128)(2,1)S(1)}, u32[]{:S(2)}, u32[]{:S(2)}) collective-permute-start(bf16[2,1,288,128]{3,2,1,0:T(8,128)(2,1)S(1)} %get-tuple-element.68), channel_id=1, source_target_pairs={{0,8},{8,0},{16,24},{24,16},{1,9},{9,1},{17,25},{25,17},{2,10},{10... | collective-permute-start | bytes 442376 | tf_op jit(solution)/shard_map/ppermute | solution.py:555
  29.3 5.2 %collective-permute-start.6 = (bf16[2,1,288,128]{3,2,1,0:T(8,128)(2,1)S(1)}, bf16[2,1,288,128]{3,2,1,0:T(8,128)(2,1)S(1)}, u32[]{:S(2)}, u32[]{:S(2)}) collective-permute-start(bf16[2,1,288,128]{3,2,1,0:T(8,128)(2,1)S(1)} %get-tuple-element.73), channel_id=1, source_target_pairs={{0,8},{8,0},{16,24},{24,16},{1,9},{9,1},{17,25},{25,17},{2,10},{10... | collective-permute-start | bytes 442376 | tf_op jit(solution)/shard_map/ppermute | solution.py:555
  34.5 14.7 %collective-permute-start.8 = (bf16[2,2,1,288,128]{4,3,2,1,0:T(8,128)(2,1)S(1)}, bf16[2,2,1,288,128]{4,3,2,1,0:T(8,128)(2,1)S(1)}, u32[]{:S(2)}, u32[]{:S(2)}) collective-permute-start(bf16[2,2,1,288,128]{4,3,2,1,0:T(8,128)(2,1)S(1)} %get-tuple-element.75.refs_0_.refs_4_), channel_id=1, source_target_pairs={{0,1},{1,0},{2,4},{4,2},{3,5},{5,3},{6,7},{7,6},{8,9},{9,8},{10,12... | collective-permute-start | bytes 884744 | tf_op jit(solution)/shard_map/ppermute | solution.py:555
  34.5 15.9 %collective-permute-start.7 = (bf16[2,2,1,288,128]{4,3,2,1,0:T(8,128)(2,1)S(1)}, bf16[2,2,1,288,128]{4,3,2,1,0:T(8,128)(2,1)S(1)}, u32[]{:S(2)}, u32[]{:S(2)}) collective-permute-start(bf16[2,2,1,288,128]{4,3,2,1,0:T(8,128)(2,1)S(1)} %get-tuple-element.75.refs_0_.refs_4_), channel_id=1, source_target_pairs={{0,2},{1,3},{2,0},{3,1},{4,6},{5,7},{6,4},{7,5},{8,10},{9,11},{10,... | collective-permute-start | bytes 884744 | tf_op jit(solution)/shard_map/ppermute | solution.py:555
  38.2 5.8 %collective-permute-start.14 = (bf16[2,1,288,128]{3,2,1,0:T(8,128)(2,1)S(1)}, bf16[2,1,288,128]{3,2,1,0:T(8,128)(2,1)S(1)}, u32[]{:S(2)}, u32[]{:S(2)}) collective-permute-start(bf16[2,1,288,128]{3,2,1,0:T(8,128)(2,1)S(1)} %get-tuple-element.89), channel_id=1, source_target_pairs={{0,8},{8,0},{16,24},{24,16},{1,9},{9,1},{17,25},{25,17},{2,10},{10... | collective-permute-start | bytes 442376 | tf_op jit(solution)/shard_map/ppermute | solution.py:555
  40.3 12.9 %collective-permute-start.12 = (bf16[2,1,288,128]{3,2,1,0:T(8,128)(2,1)S(1)}, bf16[2,1,288,128]{3,2,1,0:T(8,128)(2,1)S(1)}, u32[]{:S(2)}, u32[]{:S(2)}) collective-permute-start(bf16[2,1,288,128]{3,2,1,0:T(8,128)(2,1)S(1)} %get-tuple-element.80), channel_id=1, source_target_pairs={{0,24},{8,16},{16,8},{24,0},{1,25},{9,17},{17,9},{25,1},{2,26},{10... | collective-permute-start | bytes 442376 | tf_op jit(solution)/shard_map/ppermute | solution.py:555
  44.6 11.2 %collective-permute-start.15 = (bf16[2,1,288,128]{3,2,1,0:T(8,128)(2,1)S(1)}, bf16[2,1,288,128]{3,2,1,0:T(8,128)(2,1)S(1)}, u32[]{:S(2)}, u32[]{:S(2)}) collective-permute-start(bf16[2,1,288,128]{3,2,1,0:T(8,128)(2,1)S(1)} %get-tuple-element.93), channel_id=1, source_target_pairs={{0,24},{8,16},{16,8},{24,0},{1,25},{9,17},{17,9},{25,1},{2,26},{10... | collective-permute-start | bytes 442376 | tf_op jit(solution)/shard_map/ppermute | solution.py:555
  49.2 20.7 %collective-permute-start.9 = (bf16[2,2,1,288,128]{4,3,2,1,0:T(8,128)(2,1)S(1)}, bf16[2,2,1,288,128]{4,3,2,1,0:T(8,128)(2,1)S(1)}, u32[]{:S(2)}, u32[]{:S(2)}) collective-permute-start(bf16[2,2,1,288,128]{4,3,2,1,0:T(8,128)(2,1)S(1)} %collective-permute-done.8.refs_7_), channel_id=1, source_target_pairs={{0,2},{1,3},{2,0},{3,1},{4,6},{5,7},{6,4},{7,5},{8,10},{9,11},{10,... | collective-permute-start | bytes 884744 | tf_op jit(solution)/shard_map/ppermute | solution.py:555
  50.5 22.5 %collective-permute-start.10 = (bf16[2,2,1,288,128]{4,3,2,1,0:T(8,128)(2,1)S(1)}, bf16[2,2,1,288,128]{4,3,2,1,0:T(8,128)(2,1)}, u32[]{:S(2)}, u32[]{:S(2)}) collective-permute-start(bf16[2,2,1,288,128]{4,3,2,1,0:T(8,128)(2,1)S(1)} %get-tuple-element.75.refs_0_.refs_4_), channel_id=1, source_target_pairs={{0,6},{6,0},{1,7},{7,1},{2,3},{3,2},{4,5},{5,4},{8,14},{14,8},{9,1... | collective-permute-start | bytes 884744 | tf_op jit(solution)/shard_map/ppermute | solution.py:555
  53.1 19.8 %collective-permute-start.11 = (bf16[2,2,1,288,128]{4,3,2,1,0:T(8,128)(2,1)S(1)}, bf16[2,2,1,288,128]{4,3,2,1,0:T(8,128)(2,1)}, u32[]{:S(2)}, u32[]{:S(2)}) collective-permute-start(bf16[2,2,1,288,128]{4,3,2,1,0:T(8,128)(2,1)S(1)} %collective-permute-done.7.refs_1_.refs_5_), channel_id=1, source_target_pairs={{0,1},{1,0},{2,4},{4,2},{3,5},{5,3},{6,7},{7,6},{8,9},{9,8},{10,12... | collective-permute-start | bytes 884744 | tf_op jit(solution)/shard_map/ppermute | solution.py:555
  53.8 6.8 %collective-permute-start.13 = (bf16[2,1,288,128]{3,2,1,0:T(8,128)(2,1)S(1)}, bf16[2,1,288,128]{3,2,1,0:T(8,128)(2,1)S(1)}, u32[]{:S(2)}, u32[]{:S(2)}) collective-permute-start(bf16[2,1,288,128]{3,2,1,0:T(8,128)(2,1)S(1)} %get-tuple-element.84), channel_id=1, source_target_pairs={{0,8},{8,0},{16,24},{24,16},{1,9},{9,1},{17,25},{25,17},{2,10},{10... | collective-permute-start | bytes 442376 | tf_op jit(solution)/shard_map/ppermute | solution.py:555
  56.6 7.0 %collective-permute-start.16 = (bf16[2,1,288,128]{3,2,1,0:T(8,128)(2,1)S(1)}, bf16[2,1,288,128]{3,2,1,0:T(8,128)(2,1)S(1)}, u32[]{:S(2)}, u32[]{:S(2)}) collective-permute-start(bf16[2,1,288,128]{3,2,1,0:T(8,128)(2,1)S(1)} %get-tuple-element.97), channel_id=1, source_target_pairs={{0,8},{8,0},{16,24},{24,16},{1,9},{9,1},{17,25},{25,17},{2,10},{10... | collective-permute-start | bytes 442376 | tf_op jit(solution)/shard_map/ppermute | solution.py:555
  67.2 0.6 copy-start.5
  67.9 9.6 %collective-permute-start.17 = (bf16[400,128]{1,0:T(8,128)(2,1)}, bf16[400,128]{1,0:T(8,128)(2,1)}, u32[]{:S(2)}, u32[]{:S(2)}) collective-permute-start(bf16[400,128]{1,0:T(8,128)(2,1)} %get-tuple-element.107), channel_id=1, source_target_pairs={{0,2},{1,3},{2,0},{3,1},{4,6},{5,7},{6,4},{7,5},{8,10},{9,11},{10,... | collective-permute-start | bytes 307208 | tf_op jit(solution)/shard_map/ppermute | solution.py:555
  67.9 11.4 %collective-permute-start.18 = (bf16[400,128]{1,0:T(8,128)(2,1)}, bf16[400,128]{1,0:T(8,128)(2,1)}, u32[]{:S(2)}, u32[]{:S(2)}) collective-permute-start(bf16[400,128]{1,0:T(8,128)(2,1)} %get-tuple-element.108), channel_id=1, source_target_pairs={{0,4},{1,5},{2,6},{3,7},{4,0},{5,1},{6,2},{7,3},{8,12},{9,13},{10,... | collective-permute-start | bytes 307208 | tf_op jit(solution)/shard_map/ppermute | solution.py:555
  69.8 0.7 copy-start.3
  70.5 8.7 %collective-permute-start.19 = (bf16[400,128]{1,0:T(8,128)(2,1)}, bf16[400,128]{1,0:T(8,128)(2,1)}, u32[]{:S(2)}, u32[]{:S(2)}) collective-permute-start(bf16[400,128]{1,0:T(8,128)(2,1)} %get-tuple-element.109), channel_id=1, source_target_pairs={{0,6},{1,7},{2,4},{3,5},{4,2},{5,3},{6,0},{7,1},{8,14},{9,15},{10,... | collective-permute-start | bytes 307208 | tf_op jit(solution)/shard_map/ppermute | solution.py:555
  73.0 1.0 %copy-start.4 = (bf16[2,2,1,288,128]{4,3,2,1,0:T(8,128)(2,1)S(1)}, bf16[2,2,1,288,128]{4,3,2,1,0:T(8,128)(2,1)}, u32[]{:S(2)}) copy-start(bf16[2,2,1,288,128]{4,3,2,1,0:T(8,128)(2,1)} %copy-done.3) | copy-start | bytes 884740
  73.9 5.3 %copy-start.6 = (bf16[400,128]{1,0:T(8,128)(2,1)S(1)}, bf16[400,128]{1,0:T(8,128)(2,1)}, u32[]{:S(2)}) copy-start(bf16[400,128]{1,0:T(8,128)(2,1)} %copy-done.5) | copy-start | bytes 307204
  80.9 1.7 %collective-permute-start.20 = (bf16[336,512]{1,0:T(8,128)(2,1)S(1)}, bf16[336,512]{1,0:T(8,128)(2,1)S(1)}, u32[]{:S(2)}, u32[]{:S(2)}) collective-permute-start(bf16[336,512]{1,0:T(8,128)(2,1)S(1)} %get-tuple-element.111), channel_id=1, source_target_pairs={{0,1},{1,0},{2,3},{3,2},{4,5},{5,4},{6,7},{7,6},{8,9},{9,8},{10,11... | collective-permute-start | bytes 1032200 | tf_op jit(solution)/shard_map/ppermute | solution.py:555
